TPU v7x, 32 devices: a whole 2x2x4 slice. The times are simulated.
32 devices in a mesh: dp: 16 (over z, y, core), gz: 2 (over x).
Axes of the slice: x: 2, y: 2, z: 4, core: 2. Of those that a mesh axis runs over, the one named last changes fastest.
Arguments:
- features_in: bfloat16 [16, 32, 8, 512], P('dp', None, 'gz'), may hold values from -6 to 6
- kernel_taps: bfloat16 [27, 2048], replicated, may hold values from -0.21875 to 0.21875
- channel_bias: float32 [64], replicated, may hold values from -3 to 3
- upstream: bfloat16 [16, 64, 8, 512], P('dp', None, 'gz'), may hold values from -6 to 6
Outputs:
- output: bfloat16 [16, 64, 8, 512], P('dp', None, 'gz')
- grad_input: bfloat16 [16, 32, 8, 512], P('dp', None, 'gz')
- weight_grad: float32 [27, 2048], replicated
- bias_grad: float32 [64], replicated
All inputs are finite; a program needn't handle non-finite values.
Results may differ from a plain program's by a relative error of at most 0.0034.
Values may be sent and summed in bfloat16 or wider, within the bound.
A program may use at most 64 MiB of HBM per device.

v0:
```python
import math

import jax
import jax.numpy as jnp
from jax import lax
from jax.sharding import PartitionSpec as P

NX = 64
NY = 8


def with_halo(cells, sides, width):
    for axis, dim in sides:
        count = lax.axis_size(axis)
        ends = count - 1
        head = lax.slice_in_dim(cells, 0, width, axis=dim)
        tail = lax.slice_in_dim(cells, cells.shape[dim] - width, cells.shape[dim], axis=dim)
        cells = jnp.concatenate(
            [
                lax.ppermute(tail, axis, [(i, (i + 1) % count) for i in range(ends)]),
                cells,
                lax.ppermute(head, axis, [((i + 1) % count, i) for i in range(ends)]),
            ],
            axis=dim,
        )
    return cells


def pad_sides(field):
    return jnp.pad(field, ((0, 0), (0, 0), (0, 0), (1, 1), (1, 1)))


def correlate(field, taps):
    return lax.conv_general_dilated(
        field,
        taps,
        (1, 1, 1),
        "VALID",
        dimension_numbers=("NCDHW", "DHWIO", "NCDHW"),
        preferred_element_type=jnp.float32,
    )


def on_device(features_in, kernel_taps, channel_bias, upstream):
    in_chan = features_in.shape[1]
    out_chan = upstream.shape[1]
    vol_count = features_in.shape[0]
    planes = features_in.shape[2]
    kernel = kernel_taps.reshape(3, 3, 3, in_chan, out_chan)
    flipped = jnp.transpose(kernel[::-1, ::-1, ::-1], (0, 1, 2, 4, 3))
    feats = features_in.reshape(vol_count, in_chan, planes, NY, NX)
    grads = upstream.reshape(vol_count, out_chan, planes, NY, NX)
    padded_in = pad_sides(with_halo(feats, (("gz", 2),), 1))
    padded_up = pad_sides(with_halo(grads, (("gz", 2),), 1))
    output = (correlate(padded_in, kernel) + channel_bias[None, :, None, None, None]).astype(
        jnp.bfloat16
    )
    grad_input = correlate(padded_up, flipped).astype(jnp.bfloat16)
    weight_term = lax.conv_general_dilated(
        padded_in,
        grads,
        (1, 1, 1),
        "VALID",
        dimension_numbers=("CNDHW", "IODHW", "DHWNC"),
        preferred_element_type=jnp.float32,
    )
    weight_term = weight_term.reshape(27, in_chan * out_chan)
    bias_term = jnp.sum(grads, axis=(0, 2, 3, 4), dtype=jnp.float32)
    cells_all = vol_count * lax.axis_size("dp") * planes * lax.axis_size("gz") * NY * NX
    factor = 1.0 / math.sqrt(cells_all)
    shares = (
        lax.psum_scatter(weight_term, "gz", scatter_dimension=1, tiled=True),
        lax.psum_scatter(bias_term, "gz", scatter_dimension=0, tiled=True),
    )
    summed = lax.psum((shares[0], shares[1]), "dp")
    weight_sum, bias_sum = (
        lax.all_gather(summed[0], "gz", axis=1, tiled=True),
        lax.all_gather(summed[1], "gz", axis=0, tiled=True),
    )
    output = output.reshape(vol_count, out_chan, planes, NY * NX)
    grad_input = grad_input.reshape(vol_count, in_chan, planes, NY * NX)
    return (output, grad_input, weight_sum * factor, bias_sum * factor)


def solution(mesh):
    in_specs = (P("dp", None, "gz", None), P(), P(), P("dp", None, "gz", None))
    out_specs = (P("dp", None, "gz", None), P("dp", None, "gz", None), P(), P())
    return jax.shard_map(
        on_device, mesh=mesh, in_specs=in_specs, out_specs=out_specs, check_vma=False
    )
```

profile of v0, /device:TPU:0, one launch (start us, length us, event | category | flops | bytes accessed | tf_op | source)
XLA Modules:
  0.0 216.7 jit_solution(101169111635739117)
XLA Ops:
  7.2 0.0 reduce-scatter.2.cloned.1.call-start
  7.2 1.0 copy.71
  8.2 0.3 reshape.35
  8.5 0.7 fusion.26
  9.2 5.5 %collective-permute-start.2 = (bf16[1,64,1,8,64]{4,3,1,2,0:T(8,128)(2,1)}, bf16[1,64,1,8,64]{4,3,1,2,0:T(8,128)(2,1)}, u32[]{:S(2)}, u32[]{:S(2)}) collective-permute-start(bf16[1,64,1,8,64]{4,3,1,2,0:T(8,128)(2,1)} %get-tuple-element.18), channel_id=1, source_target_pairs={{0,1},{2,3},{4,5},{6,7},{8,9},{10,11},{12,13},{14,15},{16,17},{18,... | collective-permute-start | bytes 196616 | tf_op jit(solution)/shard_map/ppermute | solution.py:20
  14.7 1.3 collective-permute-start.3
  16.0 0.2 reshape.66
  16.2 0.0 copy-start.1
  16.2 0.0 copy-start.6
  16.2 0.8 copy.62
  17.1 0.6 fusion.25
  17.6 0.0 copy-start.5
  17.7 5.3 %collective-permute-start = (bf16[1,32,1,8,64]{1,0,4,3,2:T(2,128)(2,1)S(1)}, bf16[1,32,1,8,64]{1,0,4,3,2:T(2,128)(2,1)S(1)}, u32[]{:S(2)}, u32[]{:S(2)}) collective-permute-start(bf16[1,32,1,8,64]{1,0,4,3,2:T(2,128)(2,1)S(1)} %get-tuple-element.16), channel_id=1, source_target_pairs={{0,1},{2,3},{4,5},{6,7},{8,9},{10,11},{12,13},{14,15},{16,17},{18,... | collective-permute-start | bytes 98312 | tf_op jit(solution)/shard_map/ppermute | solution.py:20
  23.0 1.3 collective-permute-start.1
  24.3 0.6 convert_reduce_fusion
  24.9 0.0 copy-done.6
  24.9 0.6 fusion.27
  26.1 6.2 %all-reduce.1 = f32[64]{0:T(128)S(1)} all-reduce(f32[64]{0:T(128)S(1)} %convert_reduce_fusion), channel_id=3, replica_groups=mesh['dp'=16,'gz'=2] {'gz'}, use_global_device_ids=true, to_apply=%region_3.4.clone | all-reduce | flops 64 | bytes 512
  32.3 0.1 dynamic-slice.2
  32.4 32.0 %psum.15 = f32[32]{0:T(128)S(1)} all-reduce(f32[32]{0:T(128)S(1)} %dynamic-slice.2), channel_id=1, replica_groups=mesh['dp'=16,'gz'=2] {'dp'}, use_global_device_ids=true, to_apply=%region_4.5 | all-reduce | flops 32 | bytes 256 | tf_op jit(solution)/shard_map/psum | solution.py:75
  65.1 0.2 dynamic-update-slice
  65.3 4.9 %all-reduce = f32[64]{0:T(128)S(1)} all-reduce(f32[64]{0:T(128)S(1)} %dynamic-update-slice), channel_id=1, replica_groups=mesh['dp'=16,'gz'=2] {'gz'}, use_global_device_ids=true, to_apply=%add | all-reduce | flops 64 | bytes 512
  70.2 0.5 broadcast_multiply_fusion.1
  70.7 2.0 copy.77
  72.7 0.9 reshape.33
  73.6 0.0 collective-permute-done
  73.6 0.0 collective-permute-done.1
  73.6 7.0 %pad_maximum_fusion = bf16[1,32,6,8,64]{1,0,4,3,2:T(2,128)(2,1)S(1)} fusion(bf16[1,32,1,8,64]{1,0,4,3,2:T(2,128)(2,1)} %collective-permute-done.1, bf16[1,32,4,8,64]{1,0,4,3,2:T(2,128)(2,1)S(1)} %copy.62, bf16[1,32,1,8,64]{1,0,4,3,2:T(2,128)(2,1)S(1)} %collective-permute-done), kind=kLoop, calls=%fused_computation.4 | loop fusion | flops 196608 | bytes 393216 | tf_op jit(solution)/shard_map/concatenate | solution.py:18
  80.6 1.2 copy.65
  81.9 0.6 copy.86
  82.5 0.2 pad.4.clone
  82.6 0.0 copy-start.3
  82.6 0.0 copy-start.7
  82.6 0.0 copy-start.8
  82.7 0.1 copy.68
  82.8 0.1 slice.22
  82.8 0.7 copy-done.3
  83.6 0.0 copy-done.8
  83.6 2.4 %fusion.3 = bf16[4,8,8,9,64]{4,2,3,1,0:T(8,128)(2,1)S(1)} fusion(bf16[3,3,3,32,64]{4,3,2,1,0:T(8,128)(2,1)S(1)} %copy-done.3, bf16[32,6,8,1,7,2]{0,4,5,2,1,3:T(8,128)(2,1)S(1)} %slice.22, bf16[32,6,8,1,8,9]{0,4,5,2,1,3:T(8,128)(2,1)S(1)} %copy.68, f32[64]{0:T(128)S(1)} %copy-done.7, pred[8,9]{0,1:T(8,128)(4,1)S(1)} %copy-done.8), kind=kOutput, calls=%fused_computation.8 | convolution fusion | flops 234823680 | bytes 670024 | tf_op jit(solution)/shard_map/conv_general_dilated | solution.py:34
  86.0 0.0 copy-start
  86.0 0.1 copy.69
  86.1 1.1 copy-done
  87.2 12.8 %fusion.28 = f32[3,3,3,32,64]{4,3,2,1,0:T(8,128)} fusion(bf16[1,32,6,8,64]{1,0,4,3,2:T(2,128)(2,1)S(1)} %pad_maximum_fusion, bf16[1,64,4,8,64]{1,0,4,3,2:T(2,128)(2,1)S(1)} %copy-done), kind=kOutput, calls=%fused_computation.37 | convolution fusion | flops 205455360 | bytes 679936 | tf_op jit(solution)/shard_map/conv_general_dilated | solution.py:59
  100.0 1.0 copy.82
  101.0 1.0 reshape.67
  102.0 0.9 reshape.37
  102.9 0.0 reduce-scatter.2.cloned.1.call-update
  102.9 0.0 all-reduce.4.cloned.1.call-start
  103.0 0.0 collective-permute-done.2
  103.0 0.0 collective-permute-done.3
  103.0 1.1 maximum_bitcast_fusion
  104.1 0.7 copy.87
  104.8 0.2 pad.6.clone
  105.0 0.1 copy.74
  105.1 0.1 slice.26
  105.2 4.3 %fusion.4 = bf16[4,8,8,9,32]{4,2,3,1,0:T(8,128)(2,1)S(1)} fusion(bf16[3,3,3,32,64]{4,3,2,1,0:T(8,128)(2,1)S(1)} %copy-done.3, bf16[64,6,8,1,7,2]{0,4,5,2,1,3:T(8,128)(2,1)S(1)} %slice.26, bf16[64,6,8,1,8,9]{0,4,5,2,1,3:T(8,128)(2,1)S(1)} %copy.74, pred[8,9]{0,1:T(8,128)(4,1)S(1)} %copy-done.8), kind=kOutput, calls=%fused_computation.9 | convolution fusion | flops 235339776 | bytes 786504 | tf_op jit(solution)/shard_map/conv_general_dilated | solution.py:34
  109.4 0.1 copy.75
  109.5 2.2 %reduce-scatter.2.cloned.1.call-done = f32[27,1024]{1,0:T(8,128)} async-done(((f32[27,2048]{1,0:T(8,128)}), f32[27,1024]{1,0:T(8,128)}) %reduce-scatter.2.cloned.1.call-update) | async-done | bytes 110608 | tf_op jit(solution)/shard_map/reduce_scatter | solution.py:72
  111.7 0.0 all-reduce.4.cloned.1.call-update
  111.8 0.6 copy.83
  112.4 0.8 reshape.68
  113.3 89.2 %all-reduce.4.cloned.1.call-done = f32[27,1024]{1,0:T(8,128)} async-done(((f32[27,1024]{1,0:T(8,128)}), f32[27,1024]{1,0:T(8,128)}) %all-reduce.4.cloned.1.call-update) | async-done | bytes 110608 | tf_op jit(solution)/shard_map/psum | solution.py:75
  202.5 6.6 %all_gather.6 = f32[27,2048]{1,0:T(8,128)S(1)} all-gather(f32[27,1024]{1,0:T(8,128)} %all-reduce.4.cloned.1.call-done), channel_id=1, replica_groups=mesh['dp'=16,'gz'=2] {'gz'}, dimensions={1}, use_global_device_ids=true | all-gather | bytes 331776 | tf_op jit(solution)/shard_map/all_gather | solution.py:77
  209.1 0.7 broadcast_multiply_fusion
  (10 shorter events, 0.1 us)
Async XLA Ops:
  7.2 8.9 %copy-start.4 = (bf16[1,32,4,512]{3,2,1,0:T(4,128)(2,1)S(1)}, bf16[1,32,4,512]{3,2,1,0:T(4,128)(2,1)}, u32[]{:S(2)}) copy-start(bf16[1,32,4,512]{3,2,1,0:T(4,128)(2,1)} %param.4) | copy-start | bytes 393220
  7.2 104.6 %reduce-scatter.2.cloned.1.call-start = ((), (), s32[]{:S(2)}) async-start(), calls=%async_computation.1 | async-start | bytes 393216 | tf_op jit(solution)/shard_map/reduce_scatter | solution.py:72
  9.2 93.7 %collective-permute-start.2 = (bf16[1,64,1,8,64]{4,3,1,2,0:T(8,128)(2,1)}, bf16[1,64,1,8,64]{4,3,1,2,0:T(8,128)(2,1)}, u32[]{:S(2)}, u32[]{:S(2)}) collective-permute-start(bf16[1,64,1,8,64]{4,3,1,2,0:T(8,128)(2,1)} %get-tuple-element.18), channel_id=1, source_target_pairs={{0,1},{2,3},{4,5},{6,7},{8,9},{10,11},{12,13},{14,15},{16,17},{18,... | collective-permute-start | bytes 196616 | tf_op jit(solution)/shard_map/ppermute | solution.py:20
  14.7 88.2 %collective-permute-start.3 = (bf16[1,64,1,8,64]{4,3,1,2,0:T(8,128)(2,1)}, bf16[1,64,1,8,64]{4,3,1,2,0:T(8,128)(2,1)}, u32[]{:S(2)}, u32[]{:S(2)}) collective-permute-start(bf16[1,64,1,8,64]{4,3,1,2,0:T(8,128)(2,1)} %get-tuple-element.19), channel_id=1, source_target_pairs={{1,0},{3,2},{5,4},{7,6},{9,8},{11,10},{13,12},{15,14},{17,16},{19,... | collective-permute-start | bytes 196616 | tf_op jit(solution)/shard_map/ppermute | solution.py:22
  16.2 8.1 %copy-start.1 = (bf16[1,64,4,512]{3,2,1,0:T(4,128)(2,1)S(1)}, bf16[1,64,4,512]{3,2,1,0:T(4,128)(2,1)}, u32[]{:S(2)}) copy-start(bf16[1,64,4,512]{3,2,1,0:T(4,128)(2,1)} %param.7) | copy-start | bytes 786436
  16.2 8.6 %copy-start.6 = (u32[32]{0:T(128)S(1)}, u32[32]{0:T(128)}, u32[]{:S(2)}) copy-start(u32[32]{0:T(128)} %constant.21) | copy-start | bytes 388
  17.6 55.1 %copy-start.5 = (bf16[27,2048]{1,0:T(8,128)(2,1)S(1)}, bf16[27,2048]{1,0:T(8,128)(2,1)}, u32[]{:S(2)}) copy-start(bf16[27,2048]{1,0:T(8,128)(2,1)} %param.5) | copy-start | bytes 331780
  17.7 56.0 %collective-permute-start = (bf16[1,32,1,8,64]{1,0,4,3,2:T(2,128)(2,1)S(1)}, bf16[1,32,1,8,64]{1,0,4,3,2:T(2,128)(2,1)S(1)}, u32[]{:S(2)}, u32[]{:S(2)}) collective-permute-start(bf16[1,32,1,8,64]{1,0,4,3,2:T(2,128)(2,1)S(1)} %get-tuple-element.16), channel_id=1, source_target_pairs={{0,1},{2,3},{4,5},{6,7},{8,9},{10,11},{12,13},{14,15},{16,17},{18,... | collective-permute-start | bytes 98312 | tf_op jit(solution)/shard_map/ppermute | solution.py:20
  23.0 50.6 %collective-permute-start.1 = (bf16[1,32,1,8,64]{1,0,4,3,2:T(2,128)(2,1)S(1)}, bf16[1,32,1,8,64]{1,0,4,3,2:T(2,128)(2,1)}, u32[]{:S(2)}, u32[]{:S(2)}) collective-permute-start(bf16[1,32,1,8,64]{1,0,4,3,2:T(2,128)(2,1)S(1)} %get-tuple-element.17), channel_id=1, source_target_pairs={{1,0},{3,2},{5,4},{7,6},{9,8},{11,10},{13,12},{15,14},{17,16},{19,... | collective-permute-start | bytes 98312 | tf_op jit(solution)/shard_map/ppermute | solution.py:22
  82.6 0.9 copy-start.3
  82.6 0.9 copy-start.7
  82.6 0.9 copy-start.8
  86.0 1.2 copy-start
  100.0 2.0 copy-start.2
  102.9 99.6 %all-reduce.4.cloned.1.call-start = ((), (), s32[]{:S(2)}) async-start(), calls=%async_computation.2 | async-start | bytes 262144 | tf_op jit(solution)/shard_map/psum | solution.py:75
Sparse Core Ops, SparseCore 0:
  103.0 8.6 reduce-scatter.1
  115.6 86.8 all-reduce.3
where the time goes:
time: 217 us
  waiting for transfers between devices  91.5 us (42%)
  blocking collectives  49.7 us (23%)
  matrix products  19.4 us (9%)
  local copies, waits for them, and re-layouts  17 us (8%)
  between operations  15.7 us (7%)
  starting transfers between devices  13.5 us (6%)
  other arithmetic  9.9 us (5%)
    psum x1, waiting for transfers between devices, on_device(): summed = lax.psum((shares[0], shares[1]), 'dp')  89.2 us
    psum x1, blocking collectives, on_device(): summed = lax.psum((shares[0], shares[1]), 'dp')  32 us
    conv_general_dilated x1, matrix products, on_device(): lax.conv_general_dilated(padded_in, grads, (1, 1, 1), 'VALID', dimension_...  12.8 us
    unnamed x2, blocking collectives  11.1 us
    ppermute x2, starting transfers between devices, with_halo(): lax.ppermute(tail, axis, [(i, (i + 1) % count) for i in range(ends)])  10.8 us
    unnamed x29, local copies, waits for them, and re-layouts  8.53 us
    concatenate x2, other arithmetic, with_halo(): jnp.concatenate([lax.ppermute(tail, axis, [(i, (i + 1) % count) for i in...  8.11 us
    conv_general_dilated x2, matrix products, correlate(): lax.conv_general_dilated(field, taps, (1, 1, 1), 'VALID', dimension_numbe...  6.64 us
  transfers between devices with their start and end apart: 6, of which 2 were waited for; matrix products, arithmetic and copies ran while one was open for 19% of the time, Pallas kernels for 0%

commit v1 on v0

v1 whole, which is shorter than its diff:
```python
import functools
import math

import jax
import jax.numpy as jnp
from jax import lax
from jax.experimental import pallas as pl
from jax.experimental.pallas import tpu as pltpu
from jax.sharding import PartitionSpec as P

NX = 64
NY = 8
MESH = pl.DeviceIdType.MESH
LANES = 128
ROWS = 16


def shifted(plane):
    cells = plane.shape[1]
    field = plane.astype(jnp.float32)
    at = lax.broadcasted_iota(jnp.int32, (1, cells), 1)
    col = at % NX
    zero = jnp.zeros_like(field)
    sides = (
        jnp.where(col == 0, zero, pltpu.roll(field, 1, 1)),
        field,
        jnp.where(col == NX - 1, zero, pltpu.roll(field, cells - 1, 1)),
    )
    found = [jnp.where(at < NX, zero, pltpu.roll(side, NX, 1)) for side in sides]
    found += list(sides)
    found += [jnp.where(at >= cells - NX, zero, pltpu.roll(side, cells - NX, 1)) for side in sides]
    return [each.astype(jnp.bfloat16) for each in found]


def fill(buf, vol, slot, plane):
    chan = plane.shape[0]
    for tap, value in enumerate(shifted(plane)):
        buf[vol, pl.ds((slot * 9 + tap) * chan, chan), :] = value


def kernel(
    sizes, factor, x_ref, u_ref, wf_ref, wb_ref, bias_ref, out_ref, gi_ref, wg_ref,
    halo_x, halo_u, near_x, near_u, part, recv_in, acc, recv_out, gath,
    halo_send, halo_recv, in_send, in_recv, out_send, out_recv,
    gout_send, gout_recv, gin_send, gin_recv,
):
    inner_dp, n_gz, n_in, n_out = sizes
    vols, planes, in_chan, cells = x_ref.shape
    out_chan = u_ref.shape[2]
    dp, gz = lax.axis_index("dp"), lax.axis_index("gz")
    me_in = lax.rem(dp, inner_dp) * n_gz + gz
    me_out = lax.div(dp, inner_dp)

    def inner_peer(step):
        peer = lax.rem(me_in + step, n_in)
        return peer, {"dp": me_out * inner_dp + lax.div(peer, n_gz), "gz": lax.rem(peer, n_gz)}

    def outer_peer(step):
        peer = lax.rem(me_out + step, n_out)
        return peer, {"dp": peer * inner_dp + lax.rem(dp, inner_dp), "gz": gz}

    barrier = pltpu.get_barrier_semaphore()
    for step in range(1, n_in):
        pl.semaphore_signal(barrier, inc=1, device_id=inner_peer(step)[1], device_id_type=MESH)
    for step in range(1, n_out):
        pl.semaphore_signal(barrier, inc=1, device_id=outer_peer(step)[1], device_id_type=MESH)
    pl.semaphore_wait(barrier, n_in + n_out - 2)

    def halo_copies(side):
        source = planes - 1 if side == 0 else 0
        target = gz + 1 if side == 0 else gz - 1
        return [
            pltpu.make_async_remote_copy(
                src_ref=ref.at[:, source],
                dst_ref=halo.at[side],
                send_sem=halo_send.at[side, at],
                recv_sem=halo_recv.at[side, at],
                device_id={"gz": target},
                device_id_type=MESH,
            )
            for at, (ref, halo) in enumerate(((x_ref, halo_x), (u_ref, halo_u)))
        ]

    sends = (gz < n_gz - 1, gz > 0)
    gets = (gz > 0, gz < n_gz - 1)
    for side in range(2):

        @pl.when(sends[side])
        def _(side=side):
            for copy in halo_copies(side):
                copy.start()

    for vol in range(vols):
        for z in range(planes):
            fill(near_x, vol, z + 1, x_ref[vol, z])
            fill(near_u, vol, z + 1, u_ref[vol, z])

    for side in range(2):

        @pl.when(gets[side])
        def _(side=side):
            for copy in halo_copies(side):
                copy.wait_recv()

        @pl.when(jnp.logical_not(gets[side]))
        def _(side=side):
            halo_x[side] = jnp.zeros(halo_x.shape[1:], halo_x.dtype)
            halo_u[side] = jnp.zeros(halo_u.shape[1:], halo_u.dtype)

    for vol in range(vols):
        for side, slot in ((0, 0), (1, planes + 1)):
            fill(near_x, vol, slot, halo_x[side, vol])

    deep_x, deep_u = 9 * in_chan, 9 * out_chan
    term = jnp.zeros((3 * deep_x, out_chan), jnp.float32)
    bias_term = jnp.zeros((8, out_chan), jnp.float32)
    ones = jnp.ones((8, cells), jnp.bfloat16)
    lanes = (((1,), (1,)), ((), ()))
    for vol in range(vols):
        for z in range(planes):
            grad = u_ref[vol, z]
            window = near_x[vol, pl.ds(z * deep_x, 3 * deep_x), :]
            term += lax.dot_general(window, grad, lanes, preferred_element_type=jnp.float32)
            bias_term += lax.dot_general(ones, grad, lanes, preferred_element_type=jnp.float32)
    half = in_chan // 2
    term = term.reshape(27, 2, half, out_chan)
    term = jnp.concatenate([term[:, 0], term[:, 1]], axis=-1).reshape(27 * half, 2 * out_chan)
    bias_term = jnp.concatenate([bias_term, jnp.zeros_like(bias_term)], axis=-1)
    chunk = part.shape[1]
    filled = 27 * half + 8
    whole = jnp.concatenate(
        [term, bias_term, jnp.zeros((n_in * chunk - filled, LANES), jnp.float32)], axis=0
    )
    part[...] = whole.reshape(part.shape)

    def in_copy(step):
        peer, device = inner_peer(step)
        return pltpu.make_async_remote_copy(
            src_ref=part.at[peer],
            dst_ref=recv_in.at[step - 1],
            send_sem=in_send.at[step - 1],
            recv_sem=in_recv.at[step - 1],
            device_id=device,
            device_id_type=MESH,
        )

    def out_copy(step):
        peer, device = outer_peer(step)
        return pltpu.make_async_remote_copy(
            src_ref=acc.at[peer],
            dst_ref=recv_out.at[step - 1],
            send_sem=out_send.at[step - 1],
            recv_sem=out_recv.at[step - 1],
            device_id=device,
            device_id_type=MESH,
        )

    def gather_out_copy(step):
        return pltpu.make_async_remote_copy(
            src_ref=gath.at[me_in, me_out],
            dst_ref=gath.at[me_in, me_out],
            send_sem=gout_send.at[step - 1],
            recv_sem=gout_recv.at[step - 1],
            device_id=outer_peer(step)[1],
            device_id_type=MESH,
        )

    def gather_in_copy(step):
        return pltpu.make_async_remote_copy(
            src_ref=gath.at[me_in],
            dst_ref=gath.at[me_in],
            send_sem=gin_send.at[step - 1],
            recv_sem=gin_recv.at[step - 1],
            device_id=inner_peer(step)[1],
            device_id_type=MESH,
        )

    for step in range(1, n_in):
        in_copy(step).start()

    rows = (((1,), (0,)), ((), ()))
    for vol in range(vols):
        for z in range(planes):
            window = near_x[vol, pl.ds(z * deep_x, 3 * deep_x), :]
            value = lax.dot_general(wf_ref[...], window, rows, preferred_element_type=jnp.float32)
            out_ref[vol, z] = (value + bias_ref[...]).astype(jnp.bfloat16)

    for step in range(1, n_in):
        in_copy(step).wait_recv()
    total = part[me_in]
    for step in range(1, n_in):
        total += recv_in[step - 1]
    acc[...] = total.reshape(acc.shape)
    for step in range(1, n_out):
        out_copy(step).start()

    for vol in range(vols):
        for side, slot in ((0, 0), (1, planes + 1)):
            fill(near_u, vol, slot, halo_u[side, vol])
    for vol in range(vols):
        for z in range(planes):
            window = near_u[vol, pl.ds(z * deep_u, 3 * deep_u), :]
            value = lax.dot_general(wb_ref[...], window, rows, preferred_element_type=jnp.float32)
            gi_ref[vol, z] = value.astype(jnp.bfloat16)

    for step in range(1, n_out):
        out_copy(step).wait_recv()
    total = acc[me_out]
    for step in range(1, n_out):
        total += recv_out[step - 1]
    gath[me_in, me_out] = (total * factor).astype(jnp.bfloat16)
    for step in range(1, n_out):
        gather_out_copy(step).start()
    for step in range(1, n_out):
        gather_out_copy(step).wait_recv()
    for step in range(1, n_in):
        gather_in_copy(step).start()
    for step in range(1, n_in):
        gather_in_copy(step).wait_recv()
    wg_ref[...] = gath[...].reshape(wg_ref.shape)

    for side in range(2):

        @pl.when(sends[side])
        def _(side=side):
            for copy in halo_copies(side):
                copy.wait_send()

    for step in range(1, n_in):
        in_copy(step).wait_send()
        gather_in_copy(step).wait_send()
    for step in range(1, n_out):
        out_copy(step).wait_send()
        gather_out_copy(step).wait_send()


def on_device(sizes, features_in, kernel_taps, channel_bias, upstream):
    inner_dp, n_gz, n_in, n_out = sizes
    vols, in_chan, planes, cells = features_in.shape
    out_chan = upstream.shape[1]
    half = in_chan // 2
    x = features_in.reshape(vols, half, 2, planes, cells).transpose(0, 3, 2, 1, 4)
    x = x.reshape(vols, planes, in_chan, cells)
    u = upstream.transpose(0, 2, 1, 3)
    taps = kernel_taps.reshape(27, half, 2, out_chan)
    wf = taps.transpose(3, 0, 2, 1).reshape(out_chan, 27 * in_chan)
    wb = kernel_taps.reshape(27, in_chan, out_chan)[::-1].transpose(1, 0, 2)
    wb = wb.reshape(in_chan, 27 * out_chan)
    cells_all = vols * inner_dp * n_out * planes * n_gz * cells
    factor = 1.0 / math.sqrt(cells_all)
    filled = 27 * half + 8
    per = ROWS * -(-filled // (ROWS * n_in * n_out))
    vmem = pl.BlockSpec(memory_space=pltpu.VMEM)
    dma = pltpu.SemaphoreType.DMA
    steps_in, steps_out = max(n_in - 1, 1), max(n_out - 1, 1)
    out, gi, wg = pl.pallas_call(
        functools.partial(kernel, sizes, factor),
        out_shape=(
            jax.ShapeDtypeStruct((vols, planes, out_chan, cells), jnp.bfloat16),
            jax.ShapeDtypeStruct((vols, planes, in_chan, cells), jnp.bfloat16),
            jax.ShapeDtypeStruct((n_in * n_out * per, LANES), jnp.bfloat16),
        ),
        in_specs=[vmem] * 5,
        out_specs=(vmem,) * 3,
        scratch_shapes=[
            pltpu.VMEM((2, vols, in_chan, cells), jnp.bfloat16),
            pltpu.VMEM((2, vols, out_chan, cells), jnp.bfloat16),
            pltpu.VMEM((vols, (planes + 2) * 9 * in_chan, cells), jnp.bfloat16),
            pltpu.VMEM((vols, (planes + 2) * 9 * out_chan, cells), jnp.bfloat16),
            pltpu.VMEM((n_in, n_out * per, LANES), jnp.float32),
            pltpu.VMEM((steps_in, n_out * per, LANES), jnp.float32),
            pltpu.VMEM((n_out, per, LANES), jnp.float32),
            pltpu.VMEM((steps_out, per, LANES), jnp.float32),
            pltpu.VMEM((n_in, n_out, per, LANES), jnp.bfloat16),
            dma((2, 2)),
            dma((2, 2)),
            dma((steps_in,)),
            dma((steps_in,)),
            dma((steps_out,)),
            dma((steps_out,)),
            dma((steps_out,)),
            dma((steps_out,)),
            dma((steps_in,)),
            dma((steps_in,)),
        ],
        compiler_params=pltpu.CompilerParams(
            collective_id=0, has_side_effects=True, vmem_limit_bytes=56 * 2**20
        ),
    )(x, u, wf, wb, channel_bias.reshape(out_chan, 1))
    output = out.transpose(0, 2, 1, 3)
    grad_input = gi.transpose(0, 2, 1, 3)
    weight_grad = wg[: 27 * half].astype(jnp.float32).reshape(27, in_chan * out_chan)
    bias_grad = wg[27 * half, :out_chan].astype(jnp.float32)
    return (output, grad_input, weight_grad, bias_grad)


def solution(mesh):
    n_dp, n_gz = mesh.shape["dp"], mesh.shape["gz"]
    inner_dp = max(d for d in range(1, n_dp + 1) if n_dp % d == 0 and d * d <= n_dp)
    sizes = (inner_dp, n_gz, inner_dp * n_gz, n_dp // inner_dp)
    in_specs = (P("dp", None, "gz", None), P(), P(), P("dp", None, "gz", None))
    out_specs = (P("dp", None, "gz", None), P("dp", None, "gz", None), P(), P())
    return jax.shard_map(
        functools.partial(on_device, sizes),
        mesh=mesh,
        in_specs=in_specs,
        out_specs=out_specs,
        check_vma=False,
    )
```

time: 217 us -> 39.9 us (0.18)
  waiting for transfers between devices: 91.5 us -> 0 us
  blocking collectives: 49.7 us -> 0 us
  Pallas kernels: 0 us -> 28.6 us
  matrix products: 19.4 us -> 0 us
  between operations: 15.7 us -> 0.71 us
  starting transfers between devices: 13.5 us -> 0 us
  other arithmetic: 9.9 us -> 0.53 us
  local copies, waits for them, and re-layouts: 17 us -> 9.83 us
    psum x1 -> x0, waiting for transfers between devices: 89.2 us -> none  [on_device(): summed = lax.psum((shares[0], shares[1]), 'dp')]
    psum x1 -> x0, blocking collectives: 32 us -> none  [on_device(): summed = lax.psum((shares[0], shares[1]), 'dp')]
    pallas_call x0 -> x1, Pallas kernels: none -> 28.6 us  [on_device(): pl.pallas_call(functools.partial(kernel, sizes, factor), out_shape=(jax.S...]
    conv_general_dilated x3 -> x0, matrix products: 19.4 us -> none  [the longest x1 12.8 us: on_device(): lax.conv_general_dilated(padded_in, grads, (1, 1, 1), 'VALID', dimension_...]
    ppermute x4 -> x0, starting transfers between devices: 13.4 us -> none  [the longest x2 10.8 us: with_halo(): lax.ppermute(tail, axis, [(i, (i + 1) % count) for i in range(ends)])]
    unnamed x2 -> x0, blocking collectives: 11.1 us -> none
    concatenate x2 -> x0, other arithmetic: 8.11 us -> none  [with_halo(): jnp.concatenate([lax.ppermute(tail, axis, [(i, (i + 1) % count) for i in...]
    all_gather x1 -> x0, blocking collectives: 6.6 us -> none  [on_device(): lax.all_gather(summed[0], 'gz', axis=1, tiled=True)]
  transfers between devices with their start and end apart: 6 -> 0, of which waited for: 2 -> 0; matrix products, arithmetic and copies ran while one was open for 19% -> 0% of each run, Pallas kernels for 0% -> 0%
where the time goes in v1:
time: 39.9 us; the launch traced here: 39.6 us
  Pallas kernels  28.6 us (72%)
  local copies, waits for them, and re-layouts  9.83 us (25%)
  between operations  0.71 us (2%)
  other arithmetic  0.53 us (1%)
    pallas_call x1, Pallas kernels, on_device(): pl.pallas_call(functools.partial(kernel, sizes, factor), out_shape=(jax.S...  28.6 us
    unnamed x13, local copies, waits for them, and re-layouts  4.37 us
    reshape x1, local copies, waits for them, and re-layouts, on_device(): features_in.reshape(vols, half, 2, planes, cells).transpose(0, 3, 2, 1, 4)  1.64 us
    reshape x1, local copies, waits for them, and re-layouts, on_device(): wb = wb.reshape(in_chan, 27 * out_chan)  0.89 us

profile of v1, /device:TPU:0, one launch (start us, length us, event | category | flops | bytes accessed | tf_op | source)
XLA Modules:
  0.0 39.6 jit_solution(13474042655774375279)
XLA Ops:
  0.6 0.0 copy-start.4
  0.6 0.6 %copy-done.4 = f32[64]{0:T(128)S(1)} copy-done((f32[64]{0:T(128)S(1)}, f32[64]{0:T(128)}, u32[]{:S(2)}) %copy-start.4) | copy-done | bytes 280
  1.3 0.7 %copy.20.bias_ref = f32[64,1]{1,0:T(8,128)} copy(f32[64,1]{0,1:T(1,128)S(1)} %bitcast.24) | data formatting | bytes 512 | tf_op jit(solution)/shard_map/reshape | solution.py:289
  2.0 0.0 copy-start
  2.0 1.6 %copy.15 = bf16[1,16,2,4,512]{4,1,2,3,0:T(8,128)(2,1)} copy(bf16[1,16,2,4,512]{4,3,2,1,0:T(4,128)(2,1)} %bitcast.22) | data formatting | bytes 262144 | tf_op jit(solution)/shard_map/reshape | solution.py:242
  3.6 0.0 copy-done
  3.6 0.2 reshape.41
  3.8 0.1 copy.18
  3.9 0.2 rev.3
  4.1 0.9 %reshape.42.wb_ref = bf16[32,1728]{1,0:T(8,128)(2,1)} reshape(bf16[32,27,64]{2,1,0:T(8,128)(2,1)S(1)} %bitcast.18) | data formatting | bytes 221184 | tf_op jit(solution)/shard_map/reshape | solution.py:248
  5.0 0.2 reshape.39
  5.3 0.0 copy-start.1
  5.3 0.8 %copy.19.wf_ref = bf16[64,864]{1,0:T(8,128)(2,1)} copy(bf16[64,864]{0,1:T(8,128)(2,1)S(1)} %bitcast.19) | data formatting | bytes 221184 | tf_op jit(solution)/shard_map/reshape | solution.py:246
  6.1 0.2 copy-done.1
  6.2 0.7 %copy.24 = bf16[1,64,4,512]{3,1,2,0:T(8,128)(2,1)} copy(bf16[1,64,4,512]{3,2,1,0:T(4,128)(2,1)S(1)} %copy-done.1) | data formatting | bytes 524288 | tf_op args[3]
  7.0 28.6 %shard_map.75 = (bf16[1,4,64,512]{3,2,1,0:T(8,128)(2,1)}, bf16[1,4,32,512]{3,2,1,0:T(8,128)(2,1)}, bf16[512,128]{1,0:T(8,128)(2,1)}) custom-call(bf16[1,4,32,512]{3,2,1,0:T(8,128)(2,1)} %bitcast.20, bf16[1,4,64,512]{3,2,1,0:T(8,128)(2,1)} %bitcast.17, bf16[64,864]{1,0:T(8,128)(2,1)} %copy.19.wf_ref, bf16[32,1728]{1,0:T(8,128)(2,1)} %reshape.42.wb_ref, ...), custom_call_target="tpu_custom_call" | custom-call | tf_op jit(solution)/shard_map/pallas_call | solution.py:256
  35.5 0.0 copy-start.2
  35.6 1.9 %copy.21 = bf16[1,64,4,512]{3,2,1,0:T(4,128)(2,1)} copy(bf16[1,64,4,512]{3,1,2,0:T(8,128)(2,1)} %bitcast.21) | data formatting | bytes 524288
  37.4 0.0 copy-done.2
  37.5 0.0 copy-start.3
  37.5 0.8 %copy.22 = bf16[1,32,4,512]{3,2,1,0:T(4,128)(2,1)} copy(bf16[1,32,4,512]{3,1,2,0:T(8,128)(2,1)S(1)} %bitcast.23) | data formatting | bytes 262144
  38.2 0.1 copy-done.3
  38.4 0.5 %bitcast_convert_fusion = f32[64]{0:T(128)} fusion(bf16[512,128]{1,0:T(8,128)(2,1)S(1)} %copy-done.3), kind=kLoop, calls=%fused_computation.2 | loop fusion | flops 64 | bytes 384 | tf_op jit(solution)/shard_map/convert_element_type | solution.py:293
  38.9 0.7 %reshape.47 = f32[27,2048]{1,0:T(8,128)} reshape(f32[432,128]{1,0:T(8,128)S(1)} %slice_convert_fusion) | data formatting | bytes 442368 | tf_op jit(solution)/shard_map/reshape | solution.py:292
  (2 shorter events, 0.0 us)
Async XLA Ops:
  0.6 0.7 %copy-start.4 = (f32[64]{0:T(128)S(1)}, f32[64]{0:T(128)}, u32[]{:S(2)}) copy-start(f32[64]{0:T(128)} %param.6) | copy-start | bytes 772
  2.0 1.6 %copy-start = (bf16[27,2048]{1,0:T(8,128)(2,1)S(1)}, bf16[27,2048]{1,0:T(8,128)(2,1)}, u32[]{:S(2)}) copy-start(bf16[27,2048]{1,0:T(8,128)(2,1)} %param.5) | copy-start | bytes 331780
  5.3 1.0 %copy-start.1 = (bf16[1,64,4,512]{3,2,1,0:T(4,128)(2,1)S(1)}, bf16[1,64,4,512]{3,2,1,0:T(4,128)(2,1)}, u32[]{:S(2)}) copy-start(bf16[1,64,4,512]{3,2,1,0:T(4,128)(2,1)} %param.7) | copy-start | bytes 786436
  35.5 1.9 %copy-start.2 = (bf16[1,4,32,512]{3,2,1,0:T(8,128)(2,1)S(1)}, bf16[1,4,32,512]{3,2,1,0:T(8,128)(2,1)}, u32[]{:S(2)}) copy-start(bf16[1,4,32,512]{3,2,1,0:T(8,128)(2,1)} %get-tuple-element.8) | copy-start | bytes 393220
  37.5 0.9 %copy-start.3 = (bf16[512,128]{1,0:T(8,128)(2,1)S(1)}, bf16[512,128]{1,0:T(8,128)(2,1)}, u32[]{:S(2)}) copy-start(bf16[512,128]{1,0:T(8,128)(2,1)} %get-tuple-element.9) | copy-start | bytes 393220

commit v2 on v1

--- a/solution.py
+++ b/solution.py
@@ -15,10 +15,9 @@
 ROWS = 16
 
 
-def shifted(plane):
-    cells = plane.shape[1]
-    field = plane.astype(jnp.float32)
-    at = lax.broadcasted_iota(jnp.int32, (1, cells), 1)
+def shifted(field):
+    cells = field.shape[1]
+    at = lax.broadcasted_iota(jnp.int32, field.shape, 1)
     col = at % NX
     zero = jnp.zeros_like(field)
     sides = (
@@ -32,21 +31,22 @@
     return [each.astype(jnp.bfloat16) for each in found]
 
 
-def fill(buf, vol, slot, plane):
-    chan = plane.shape[0]
-    for tap, value in enumerate(shifted(plane)):
-        buf[vol, pl.ds((slot * 9 + tap) * chan, chan), :] = value
+def fill(buf, vol, slot, chan, piece, field):
+    for tap, value in enumerate(shifted(field)):
+        buf[vol, pl.ds((slot * 9 + tap) * chan + piece * ROWS, ROWS), :] = value
 
 
 def kernel(
-    sizes, factor, x_ref, u_ref, wf_ref, wb_ref, bias_ref, out_ref, gi_ref, wg_ref,
-    halo_x, halo_u, near_x, near_u, part, recv_in, acc, recv_out, gath,
+    sizes, factor, x_ref, u_ref, taps_ref, bias_ref, out_ref, gi_ref, wg_ref, bg_ref,
+    rows_x, rows_u, edge_x, edge_u, taps_rows, wf, wb,
+    halo_x, halo_u, near_x, near_u, part, recv_in, acc, recv_out, gath, sums,
     halo_send, halo_recv, in_send, in_recv, out_send, out_recv,
     gout_send, gout_recv, gin_send, gin_recv,
 ):
     inner_dp, n_gz, n_in, n_out = sizes
-    vols, planes, in_chan, cells = x_ref.shape
-    out_chan = u_ref.shape[2]
+    vols, in_chan, planes, cells = x_ref.shape
+    out_chan = u_ref.shape[1]
+    half = in_chan // 2
     dp, gz = lax.axis_index("dp"), lax.axis_index("gz")
     me_in = lax.rem(dp, inner_dp) * n_gz + gz
     me_out = lax.div(dp, inner_dp)
@@ -59,26 +59,65 @@
         peer = lax.rem(me_out + step, n_out)
         return peer, {"dp": peer * inner_dp + lax.rem(dp, inner_dp), "gz": gz}
 
+    tiles = cells // LANES
+
+    def piece_x(vol, z, piece):
+        at = pl.ds(piece * planes + z, half, stride=2 * planes)
+        return jnp.concatenate([rows_x[vol, tile, at, :] for tile in range(tiles)], axis=1)
+
+    def piece_u(vol, z, piece):
+        at = pl.ds(piece * ROWS * planes + z, ROWS, stride=planes)
+        return jnp.concatenate([rows_u[vol, tile, at, :] for tile in range(tiles)], axis=1)
+
+    def spread(rows, vol, ref, chan):
+        for i in range(chan):
+            value = ref[vol, i].astype(jnp.float32)
+            for tile in range(tiles):
+                at = slice(tile * LANES, (tile + 1) * LANES)
+                rows[vol, tile, pl.ds(i * planes, planes), :] = value[:, at]
+
+    def put(rows, vol, at, value):
+        for tile in range(tiles):
+            rows[vol, tile, at, :] = value[:, tile * LANES : (tile + 1) * LANES]
+
+    def unite(rows, vol, ref, chan):
+        for i in range(chan):
+            at = pl.ds(i * planes, planes)
+            value = jnp.concatenate([rows[vol, tile, at, :] for tile in range(tiles)], axis=1)
+            ref[vol, i] = value.astype(jnp.bfloat16)
+
     barrier = pltpu.get_barrier_semaphore()
     for step in range(1, n_in):
         pl.semaphore_signal(barrier, inc=1, device_id=inner_peer(step)[1], device_id_type=MESH)
     for step in range(1, n_out):
         pl.semaphore_signal(barrier, inc=1, device_id=outer_peer(step)[1], device_id_type=MESH)
+
+    for vol in range(vols):
+        spread(rows_x, vol, x_ref, in_chan)
+        spread(rows_u, vol, u_ref, out_chan)
+        for side, z in ((0, planes - 1), (1, 0)):
+            for piece in range(2):
+                at = pl.ds(piece * half, half)
+                edge_x[side, vol, at, :] = piece_x(vol, z, piece).astype(jnp.bfloat16)
+            for piece in range(out_chan // ROWS):
+                at = pl.ds(piece * ROWS, ROWS)
+                edge_u[side, vol, at, :] = piece_u(vol, z, piece).astype(jnp.bfloat16)
+
     pl.semaphore_wait(barrier, n_in + n_out - 2)
 
-    def halo_copies(side):
-        source = planes - 1 if side == 0 else 0
+    def halo_copies(side, which=(0, 1)):
         target = gz + 1 if side == 0 else gz - 1
         return [
             pltpu.make_async_remote_copy(
-                src_ref=ref.at[:, source],
+                src_ref=ref.at[side],
                 dst_ref=halo.at[side],
                 send_sem=halo_send.at[side, at],
                 recv_sem=halo_recv.at[side, at],
                 device_id={"gz": target},
                 device_id_type=MESH,
             )
-            for at, (ref, halo) in enumerate(((x_ref, halo_x), (u_ref, halo_u)))
+            for at, (ref, halo) in enumerate(((edge_x, halo_x), (edge_u, halo_u)))
+            if at in which
         ]
 
     sends = (gz < n_gz - 1, gz > 0)
@@ -90,17 +129,40 @@
             for copy in halo_copies(side):
                 copy.start()
 
+    deep_x, deep_u = 9 * in_chan, 9 * out_chan
+    lanes = (((1,), (1,)), ((), ()))
     for vol in range(vols):
         for z in range(planes):
-            fill(near_x, vol, z + 1, x_ref[vol, z])
-            fill(near_u, vol, z + 1, u_ref[vol, z])
+            for piece in range(2):
+                fill(near_x, vol, z + 1, in_chan, piece, piece_x(vol, z, piece))
+            for piece in range(out_chan // ROWS):
+                fill(near_u, vol, z + 1, out_chan, piece, piece_u(vol, z, piece))
+
+    ones = jnp.ones((8, cells), jnp.bfloat16)
+    bias_term = jnp.zeros((8, out_chan), jnp.float32)
+    terms = [jnp.zeros((deep_x, out_chan), jnp.float32) for _ in range(3)]
+
+    def grad(vol, z):
+        return near_u[vol, pl.ds(((z + 1) * 9 + 4) * out_chan, out_chan), :]
+
+    def pair(vol, z, tap):
+        window = near_x[vol, pl.ds((z + tap) * deep_x, deep_x), :]
+        return lax.dot_general(window, grad(vol, z), lanes, preferred_element_type=jnp.float32)
+
+    for vol in range(vols):
+        for z in range(planes):
+            bias_term += lax.dot_general(
+                ones, grad(vol, z), lanes, preferred_element_type=jnp.float32
+            )
+            for tap in range(3):
+                if 1 <= z + tap <= planes:
+                    terms[tap] += pair(vol, z, tap)
 
     for side in range(2):
 
         @pl.when(gets[side])
         def _(side=side):
-            for copy in halo_copies(side):
-                copy.wait_recv()
+            halo_copies(side, (0,))[0].wait_recv()
 
         @pl.when(jnp.logical_not(gets[side]))
         def _(side=side):
@@ -109,20 +171,12 @@
 
     for vol in range(vols):
         for side, slot in ((0, 0), (1, planes + 1)):
-            fill(near_x, vol, slot, halo_x[side, vol])
-
-    deep_x, deep_u = 9 * in_chan, 9 * out_chan
-    term = jnp.zeros((3 * deep_x, out_chan), jnp.float32)
-    bias_term = jnp.zeros((8, out_chan), jnp.float32)
-    ones = jnp.ones((8, cells), jnp.bfloat16)
-    lanes = (((1,), (1,)), ((), ()))
-    for vol in range(vols):
-        for z in range(planes):
-            grad = u_ref[vol, z]
-            window = near_x[vol, pl.ds(z * deep_x, 3 * deep_x), :]
-            term += lax.dot_general(window, grad, lanes, preferred_element_type=jnp.float32)
-            bias_term += lax.dot_general(ones, grad, lanes, preferred_element_type=jnp.float32)
-    half = in_chan // 2
+            for piece in range(2):
+                field = halo_x[side, vol, pl.ds(piece * half, half), :].astype(jnp.float32)
+                fill(near_x, vol, slot, in_chan, piece, field)
+        terms[0] += pair(vol, 0, 0)
+        terms[2] += pair(vol, planes - 1, 2)
+    term = jnp.concatenate(terms, axis=0)
     term = term.reshape(27, 2, half, out_chan)
     term = jnp.concatenate([term[:, 0], term[:, 1]], axis=-1).reshape(27 * half, 2 * out_chan)
     bias_term = jnp.concatenate([bias_term, jnp.zeros_like(bias_term)], axis=-1)
@@ -178,12 +232,32 @@
     for step in range(1, n_in):
         in_copy(step).start()
 
+    stride = taps_rows.shape[0] // half
+    for j in range(half):
+        taps_rows[pl.ds(j * stride, 27), :] = taps_ref[:, pl.ds(j * LANES, LANES)].astype(jnp.float32)
+
+    def tap_kernel(t):
+        both = taps_rows[pl.ds(t, half, stride=stride), :]
+        return jnp.concatenate([both[:, :out_chan], both[:, out_chan:]], axis=0)
+
+    group = LANES // in_chan
+    for t in range(0, 27, group):
+        some = jnp.concatenate([tap_kernel(t + k) for k in range(min(group, 27 - t))], axis=0)
+        wf[:, pl.ds(t * in_chan, some.shape[0])] = some.T.astype(jnp.bfloat16)
+    for t in range(0, 27, 2):
+        some = [tap_kernel(26 - t - k) for k in range(min(2, 27 - t))]
+        some = jnp.concatenate(some, axis=1)
+        wb[:, pl.ds(t * out_chan, some.shape[1])] = some.astype(jnp.bfloat16)
+
     rows = (((1,), (0,)), ((), ()))
+    bias = jnp.broadcast_to(bias_ref[...], (LANES, out_chan)).T
+    bias = jnp.concatenate([bias] * (cells // LANES), axis=1)
     for vol in range(vols):
         for z in range(planes):
             window = near_x[vol, pl.ds(z * deep_x, 3 * deep_x), :]
-            value = lax.dot_general(wf_ref[...], window, rows, preferred_element_type=jnp.float32)
-            out_ref[vol, z] = (value + bias_ref[...]).astype(jnp.bfloat16)
+            value = lax.dot_general(wf[...], window, rows, preferred_element_type=jnp.float32)
+            put(rows_u, vol, pl.ds(z, out_chan, stride=planes), value + bias)
+        unite(rows_u, vol, out_ref, out_chan)
 
     for step in range(1, n_in):
         in_copy(step).wait_recv()
@@ -194,14 +268,25 @@
     for step in range(1, n_out):
         out_copy(step).start()
 
+    for side in range(2):
+
+        @pl.when(gets[side])
+        def _(side=side):
+            halo_copies(side, (1,))[0].wait_recv()
+
     for vol in range(vols):
         for side, slot in ((0, 0), (1, planes + 1)):
-            fill(near_u, vol, slot, halo_u[side, vol])
+            for piece in range(out_chan // ROWS):
+                field = halo_u[side, vol, pl.ds(piece * ROWS, ROWS), :].astype(jnp.float32)
+                fill(near_u, vol, slot, out_chan, piece, field)
     for vol in range(vols):
         for z in range(planes):
             window = near_u[vol, pl.ds(z * deep_u, 3 * deep_u), :]
-            value = lax.dot_general(wb_ref[...], window, rows, preferred_element_type=jnp.float32)
-            gi_ref[vol, z] = value.astype(jnp.bfloat16)
+            value = lax.dot_general(wb[...], window, rows, preferred_element_type=jnp.float32)
+            for piece in range(2):
+                at = pl.ds(piece * planes + z, half, stride=2 * planes)
+                put(rows_x, vol, at, value[piece * half : (piece + 1) * half])
+        unite(rows_x, vol, gi_ref, in_chan)
 
     for step in range(1, n_out):
         out_copy(step).wait_recv()
@@ -217,7 +302,10 @@
         gather_in_copy(step).start()
     for step in range(1, n_in):
         gather_in_copy(step).wait_recv()
-    wg_ref[...] = gath[...].reshape(wg_ref.shape)
+    sums[...] = gath[...].astype(jnp.float32).reshape(sums.shape)
+    for j in range(half):
+        wg_ref[:, pl.ds(j * LANES, LANES)] = sums[pl.ds(j, 27, stride=half), :]
+    bg_ref[...] = sums[pl.ds(27 * half, 1), :out_chan]
 
     for side in range(2):
 
@@ -239,13 +327,6 @@
     vols, in_chan, planes, cells = features_in.shape
     out_chan = upstream.shape[1]
     half = in_chan // 2
-    x = features_in.reshape(vols, half, 2, planes, cells).transpose(0, 3, 2, 1, 4)
-    x = x.reshape(vols, planes, in_chan, cells)
-    u = upstream.transpose(0, 2, 1, 3)
-    taps = kernel_taps.reshape(27, half, 2, out_chan)
-    wf = taps.transpose(3, 0, 2, 1).reshape(out_chan, 27 * in_chan)
-    wb = kernel_taps.reshape(27, in_chan, out_chan)[::-1].transpose(1, 0, 2)
-    wb = wb.reshape(in_chan, 27 * out_chan)
     cells_all = vols * inner_dp * n_out * planes * n_gz * cells
     factor = 1.0 / math.sqrt(cells_all)
     filled = 27 * half + 8
@@ -253,16 +334,24 @@
     vmem = pl.BlockSpec(memory_space=pltpu.VMEM)
     dma = pltpu.SemaphoreType.DMA
     steps_in, steps_out = max(n_in - 1, 1), max(n_out - 1, 1)
-    out, gi, wg = pl.pallas_call(
+    output, grad_input, weight_grad, bias_grad = pl.pallas_call(
         functools.partial(kernel, sizes, factor),
         out_shape=(
-            jax.ShapeDtypeStruct((vols, planes, out_chan, cells), jnp.bfloat16),
-            jax.ShapeDtypeStruct((vols, planes, in_chan, cells), jnp.bfloat16),
-            jax.ShapeDtypeStruct((n_in * n_out * per, LANES), jnp.bfloat16),
+            jax.ShapeDtypeStruct(upstream.shape, jnp.bfloat16),
+            jax.ShapeDtypeStruct(features_in.shape, jnp.bfloat16),
+            jax.ShapeDtypeStruct(kernel_taps.shape, jnp.float32),
+            jax.ShapeDtypeStruct((1, out_chan), jnp.float32),
         ),
-        in_specs=[vmem] * 5,
-        out_specs=(vmem,) * 3,
+        in_specs=[vmem] * 4,
+        out_specs=(vmem,) * 4,
         scratch_shapes=[
+            pltpu.VMEM((vols, cells // LANES, in_chan * planes, LANES), jnp.float32),
+            pltpu.VMEM((vols, cells // LANES, out_chan * planes, LANES), jnp.float32),
+            pltpu.VMEM((2, vols, in_chan, cells), jnp.bfloat16),
+            pltpu.VMEM((2, vols, out_chan, cells), jnp.bfloat16),
+            pltpu.VMEM((32 * half, LANES), jnp.float32),
+            pltpu.VMEM((out_chan, 27 * in_chan), jnp.bfloat16),
+            pltpu.VMEM((in_chan, 27 * out_chan), jnp.bfloat16),
             pltpu.VMEM((2, vols, in_chan, cells), jnp.bfloat16),
             pltpu.VMEM((2, vols, out_chan, cells), jnp.bfloat16),
             pltpu.VMEM((vols, (planes + 2) * 9 * in_chan, cells), jnp.bfloat16),
@@ -272,6 +361,7 @@
             pltpu.VMEM((n_out, per, LANES), jnp.float32),
             pltpu.VMEM((steps_out, per, LANES), jnp.float32),
             pltpu.VMEM((n_in, n_out, per, LANES), jnp.bfloat16),
+            pltpu.VMEM((n_in * n_out * per, LANES), jnp.float32),
             dma((2, 2)),
             dma((2, 2)),
             dma((steps_in,)),
@@ -286,12 +376,8 @@
         compiler_params=pltpu.CompilerParams(
             collective_id=0, has_side_effects=True, vmem_limit_bytes=56 * 2**20
         ),
-    )(x, u, wf, wb, channel_bias.reshape(out_chan, 1))
-    output = out.transpose(0, 2, 1, 3)
-    grad_input = gi.transpose(0, 2, 1, 3)
-    weight_grad = wg[: 27 * half].astype(jnp.float32).reshape(27, in_chan * out_chan)
-    bias_grad = wg[27 * half, :out_chan].astype(jnp.float32)
-    return (output, grad_input, weight_grad, bias_grad)
+    )(features_in, upstream, kernel_taps, channel_bias.reshape(1, out_chan))
+    return (output, grad_input, weight_grad, bias_grad.reshape(out_chan))
 
 
 def solution(mesh):

time: 39.9 us -> 30.9 us (0.77)
  local copies, waits for them, and re-layouts: 9.83 us -> 3.67 us
  Pallas kernels: 28.6 us -> 26.5 us
  other arithmetic: 0.53 us -> 0 us
    reshape x9 -> x0, local copies, waits for them, and re-layouts: 5.27 us -> none  [the longest x1 1.64 us: on_device(): features_in.reshape(vols, half, 2, planes, cells).transpose(0, 3, 2, 1, 4)]
    pallas_call x1, Pallas kernels: 28.6 us -> 26.5 us  [on_device(): pl.pallas_call(functools.partial(kernel, sizes, factor), out_shape=(jax.S...]
    unnamed x13 -> x10, local copies, waits for them, and re-layouts: 4.37 us -> 3.67 us
    convert_element_type x1 -> x0, other arithmetic: 0.51 us -> none  [on_device(): bias_grad = wg[27 * half, :out_chan].astype(jnp.float32)]
where the time goes in v2:
time: 30.9 us; the launch traced here: 30.8 us
  Pallas kernels  26.5 us (86%)
  local copies, waits for them, and re-layouts  3.67 us (12%)
  between operations  0.66 us (2%)
    pallas_call x1, Pallas kernels, on_device(): pl.pallas_call(functools.partial(kernel, sizes, factor), out_shape=(jax.S...  26.5 us
    unnamed x10, local copies, waits for them, and re-layouts  3.67 us

profile of v2, /device:TPU:0, one launch (start us, length us, event | category | flops | bytes accessed | tf_op | source)
XLA Modules:
  0.0 30.8 jit_solution(2293625683474802287)
XLA Ops:
  0.6 26.5 %shard_map.75 = (bf16[1,64,4,512]{3,2,1,0:T(4,128)(2,1)}, bf16[1,32,4,512]{3,2,1,0:T(4,128)(2,1)}, f32[27,2048]{1,0:T(8,128)}, f32[1,64]{1,0:T(1,128)}) custom-call(bf16[1,32,4,512]{3,2,1,0:T(4,128)(2,1)} %x_ref.1, bf16[1,64,4,512]{3,2,1,0:T(4,128)(2,1)} %u_ref.1, bf16[27,2048]{1,0:T(8,128)(2,1)} %taps_ref.1, f32[1,64]{1,0:T(1,128)} %bitcast.2), custom_call_target="tpu_custom_call" | custom-call | tf_op jit(solution)/shard_map/pallas_call | solution.py:337
  27.1 0.0 copy-start.1
  27.1 0.0 copy-start
  27.1 1.8 %copy.12 = bf16[1,64,4,512]{3,2,1,0:T(4,128)(2,1)} copy(bf16[1,64,4,512]{3,2,1,0:T(4,128)(2,1)} %get-tuple-element.16) | data formatting | bytes 524288
  28.9 0.0 copy-done.1
  28.9 0.7 %copy.13 = bf16[1,32,4,512]{3,2,1,0:T(4,128)(2,1)} copy(bf16[1,32,4,512]{3,2,1,0:T(4,128)(2,1)S(1)} %copy-done.1) | data formatting | bytes 262144
  29.6 0.0 copy-done
  29.6 0.0 copy-start.2
  29.6 0.7 %copy.14 = f32[27,2048]{1,0:T(8,128)} copy(f32[27,2048]{1,0:T(8,128)S(1)} %copy-done) | data formatting | bytes 442368
  30.3 0.0 copy-done.2
  30.3 0.5 %copy.15 = f32[64]{0:T(128)} copy(f32[64]{0:T(128)S(1)} %bitcast.3) | data formatting | bytes 512
Async XLA Ops:
  27.1 1.8 %copy-start.1 = (bf16[1,32,4,512]{3,2,1,0:T(4,128)(2,1)S(1)}, bf16[1,32,4,512]{3,2,1,0:T(4,128)(2,1)}, u32[]{:S(2)}) copy-start(bf16[1,32,4,512]{3,2,1,0:T(4,128)(2,1)} %get-tuple-element.17) | copy-start | bytes 393220
  27.1 2.5 %copy-start = (f32[27,2048]{1,0:T(8,128)S(1)}, f32[27,2048]{1,0:T(8,128)}, u32[]{:S(2)}) copy-start(f32[27,2048]{1,0:T(8,128)} %get-tuple-element.18) | copy-start | bytes 663556
  29.6 0.7 %copy-start.2 = (f32[1,64]{1,0:T(1,128)S(1)}, f32[1,64]{1,0:T(1,128)}, u32[]{:S(2)}) copy-start(f32[1,64]{1,0:T(1,128)} %get-tuple-element.11) | copy-start | bytes 772

commit v3 on v2

--- a/solution.py
+++ b/solution.py
@@ -31,14 +31,18 @@
     return [each.astype(jnp.bfloat16) for each in found]
 
 
-def fill(buf, vol, slot, chan, piece, field):
+def fill(buf, vol, start, chan, piece, field):
     for tap, value in enumerate(shifted(field)):
-        buf[vol, pl.ds((slot * 9 + tap) * chan + piece * ROWS, ROWS), :] = value
+        buf[vol, pl.ds(start + tap * chan + piece * ROWS, ROWS), :] = value
+
+
+def depth(chan):
+    return LANES * -(-9 * chan // LANES)
 
 
 def kernel(
-    sizes, factor, x_ref, u_ref, taps_ref, bias_ref, out_ref, gi_ref, wg_ref, bg_ref,
-    rows_x, rows_u, edge_x, edge_u, taps_rows, wf, wb,
+    sizes, factor, x_hbm, u_hbm, taps_hbm, bias_ref, out_ref, gi_ref, wg_ref, bg_ref,
+    x_ref, u_ref, taps_ref, load, rows_x, rows_u, edge_x, edge_u, taps_rows, wf, wb,
     halo_x, halo_u, near_x, near_u, part, recv_in, acc, recv_out, gath, sums,
     halo_send, halo_recv, in_send, in_recv, out_send, out_recv,
     gout_send, gout_recv, gin_send, gin_recv,
@@ -86,22 +90,26 @@
             value = jnp.concatenate([rows[vol, tile, at, :] for tile in range(tiles)], axis=1)
             ref[vol, i] = value.astype(jnp.bfloat16)
 
+    loads = [
+        pltpu.make_async_copy(source, target, load.at[at])
+        for at, (source, target) in enumerate(((x_hbm, x_ref), (u_hbm, u_ref), (taps_hbm, taps_ref)))
+    ]
+    for copy in loads:
+        copy.start()
     barrier = pltpu.get_barrier_semaphore()
     for step in range(1, n_in):
         pl.semaphore_signal(barrier, inc=1, device_id=inner_peer(step)[1], device_id_type=MESH)
     for step in range(1, n_out):
         pl.semaphore_signal(barrier, inc=1, device_id=outer_peer(step)[1], device_id_type=MESH)
 
+    deep_x, deep_u = 9 * in_chan, depth(out_chan)
+    loads[0].wait()
     for vol in range(vols):
         spread(rows_x, vol, x_ref, in_chan)
-        spread(rows_u, vol, u_ref, out_chan)
         for side, z in ((0, planes - 1), (1, 0)):
             for piece in range(2):
                 at = pl.ds(piece * half, half)
                 edge_x[side, vol, at, :] = piece_x(vol, z, piece).astype(jnp.bfloat16)
-            for piece in range(out_chan // ROWS):
-                at = pl.ds(piece * ROWS, ROWS)
-                edge_u[side, vol, at, :] = piece_u(vol, z, piece).astype(jnp.bfloat16)
 
     pl.semaphore_wait(barrier, n_in + n_out - 2)
 
@@ -122,28 +130,39 @@
 
     sends = (gz < n_gz - 1, gz > 0)
     gets = (gz > 0, gz < n_gz - 1)
-    for side in range(2):
-
-        @pl.when(sends[side])
-        def _(side=side):
-            for copy in halo_copies(side):
-                copy.start()
-
-    deep_x, deep_u = 9 * in_chan, 9 * out_chan
+    def send_halos(which):
+        for side in range(2):
+
+            @pl.when(sends[side])
+            def _(side=side):
+                halo_copies(side, (which,))[0].start()
+
+    def center(slot):
+        return slot * deep_u + 4 * out_chan
+
+    send_halos(0)
+    loads[1].wait()
+    for vol in range(vols):
+        spread(rows_u, vol, u_ref, out_chan)
+        for z in range(planes):
+            for piece in range(out_chan // ROWS):
+                value = piece_u(vol, z, piece).astype(jnp.bfloat16)
+                near_u[vol, pl.ds(center(z + 1) + piece * ROWS, ROWS), :] = value
+        for side, z in ((0, planes - 1), (1, 0)):
+            edge_u[side, vol] = near_u[vol, pl.ds(center(z + 1), out_chan), :]
+    send_halos(1)
     lanes = (((1,), (1,)), ((), ()))
     for vol in range(vols):
         for z in range(planes):
             for piece in range(2):
-                fill(near_x, vol, z + 1, in_chan, piece, piece_x(vol, z, piece))
-            for piece in range(out_chan // ROWS):
-                fill(near_u, vol, z + 1, out_chan, piece, piece_u(vol, z, piece))
+                fill(near_x, vol, (z + 1) * deep_x, in_chan, piece, piece_x(vol, z, piece))
 
     ones = jnp.ones((8, cells), jnp.bfloat16)
     bias_term = jnp.zeros((8, out_chan), jnp.float32)
     terms = [jnp.zeros((deep_x, out_chan), jnp.float32) for _ in range(3)]
 
     def grad(vol, z):
-        return near_u[vol, pl.ds(((z + 1) * 9 + 4) * out_chan, out_chan), :]
+        return near_u[vol, pl.ds(center(z + 1), out_chan), :]
 
     def pair(vol, z, tap):
         window = near_x[vol, pl.ds((z + tap) * deep_x, deep_x), :]
@@ -173,7 +192,7 @@
         for side, slot in ((0, 0), (1, planes + 1)):
             for piece in range(2):
                 field = halo_x[side, vol, pl.ds(piece * half, half), :].astype(jnp.float32)
-                fill(near_x, vol, slot, in_chan, piece, field)
+                fill(near_x, vol, slot * deep_x, in_chan, piece, field)
         terms[0] += pair(vol, 0, 0)
         terms[2] += pair(vol, planes - 1, 2)
     term = jnp.concatenate(terms, axis=0)
@@ -232,6 +251,7 @@
     for step in range(1, n_in):
         in_copy(step).start()
 
+    loads[2].wait()
     stride = taps_rows.shape[0] // half
     for j in range(half):
         taps_rows[pl.ds(j * stride, 27), :] = taps_ref[:, pl.ds(j * LANES, LANES)].astype(jnp.float32)
@@ -244,10 +264,24 @@
     for t in range(0, 27, group):
         some = jnp.concatenate([tap_kernel(t + k) for k in range(min(group, 27 - t))], axis=0)
         wf[:, pl.ds(t * in_chan, some.shape[0])] = some.T.astype(jnp.bfloat16)
-    for t in range(0, 27, 2):
-        some = [tap_kernel(26 - t - k) for k in range(min(2, 27 - t))]
-        some = jnp.concatenate(some, axis=1)
-        wb[:, pl.ds(t * out_chan, some.shape[1])] = some.astype(jnp.bfloat16)
+    wb[...] = jnp.zeros_like(wb)
+    for a in range(3):
+        for t in range(0, 9, 2):
+            some = [tap_kernel(26 - 9 * a - t - k) for k in range(min(2, 9 - t))]
+            some = jnp.concatenate(some, axis=1).astype(jnp.bfloat16)
+            for z in range(planes):
+                at = pl.ds((z + a) * deep_u + t * out_chan, some.shape[1])
+                wb[pl.ds(z * in_chan, in_chan), at] = some
+
+    pad = deep_u - 9 * out_chan
+    for vol in range(vols):
+        if pad:
+            for slot in range(planes + 2):
+                at = pl.ds(slot * deep_u + 9 * out_chan, pad)
+                near_u[vol, at, :] = jnp.zeros((pad, cells), jnp.bfloat16)
+        for z in range(planes):
+            for piece in range(out_chan // ROWS):
+                fill(near_u, vol, (z + 1) * deep_u, out_chan, piece, piece_u(vol, z, piece))
 
     rows = (((1,), (0,)), ((), ()))
     bias = jnp.broadcast_to(bias_ref[...], (LANES, out_chan)).T
@@ -257,8 +291,6 @@
             window = near_x[vol, pl.ds(z * deep_x, 3 * deep_x), :]
             value = lax.dot_general(wf[...], window, rows, preferred_element_type=jnp.float32)
             put(rows_u, vol, pl.ds(z, out_chan, stride=planes), value + bias)
-        unite(rows_u, vol, out_ref, out_chan)
-
     for step in range(1, n_in):
         in_copy(step).wait_recv()
     total = part[me_in]
@@ -278,15 +310,23 @@
         for side, slot in ((0, 0), (1, planes + 1)):
             for piece in range(out_chan // ROWS):
                 field = halo_u[side, vol, pl.ds(piece * ROWS, ROWS), :].astype(jnp.float32)
-                fill(near_u, vol, slot, out_chan, piece, field)
-    for vol in range(vols):
-        for z in range(planes):
-            window = near_u[vol, pl.ds(z * deep_u, 3 * deep_u), :]
-            value = lax.dot_general(wb[...], window, rows, preferred_element_type=jnp.float32)
-            for piece in range(2):
-                at = pl.ds(piece * planes + z, half, stride=2 * planes)
-                put(rows_x, vol, at, value[piece * half : (piece + 1) * half])
-        unite(rows_x, vol, gi_ref, in_chan)
+                fill(near_u, vol, slot * deep_u, out_chan, piece, field)
+    for vol in range(vols):
+        unite(rows_u, vol, out_ref, out_chan)
+
+    def backward(first):
+        tile = min(2 * LANES, cells)
+        for vol in range(vols):
+            for at in range(0 if first else tile, tile if first else cells, tile):
+                field = near_u[vol, :, pl.ds(at, tile)]
+                value = lax.dot_general(wb[...], field, rows, preferred_element_type=jnp.float32)
+                for z in range(planes):
+                    for piece in range(2):
+                        low = z * in_chan + piece * half
+                        out = pl.ds(piece * planes + z, half, stride=2 * planes)
+                        for k in range(tile // LANES):
+                            part_k = value[low : low + half, k * LANES : (k + 1) * LANES]
+                            rows_x[vol, at // LANES + k, out, :] = part_k
 
     for step in range(1, n_out):
         out_copy(step).wait_recv()
@@ -296,10 +336,14 @@
     gath[me_in, me_out] = (total * factor).astype(jnp.bfloat16)
     for step in range(1, n_out):
         gather_out_copy(step).start()
+    backward(True)
     for step in range(1, n_out):
         gather_out_copy(step).wait_recv()
     for step in range(1, n_in):
         gather_in_copy(step).start()
+    backward(False)
+    for vol in range(vols):
+        unite(rows_x, vol, gi_ref, in_chan)
     for step in range(1, n_in):
         gather_in_copy(step).wait_recv()
     sums[...] = gath[...].astype(jnp.float32).reshape(sums.shape)
@@ -320,6 +364,15 @@
     for step in range(1, n_out):
         out_copy(step).wait_send()
         gather_out_copy(step).wait_send()
+
+
+def finish(*refs):
+    sem = refs[8]
+    copies = [pltpu.make_async_copy(refs[k], refs[4 + k], sem.at[k]) for k in range(4)]
+    for copy in copies:
+        copy.start()
+    for copy in copies:
+        copy.wait()
 
 
 def on_device(sizes, features_in, kernel_taps, channel_bias, upstream):
@@ -332,9 +385,45 @@
     filled = 27 * half + 8
     per = ROWS * -(-filled // (ROWS * n_in * n_out))
     vmem = pl.BlockSpec(memory_space=pltpu.VMEM)
+    hbm = pl.BlockSpec(memory_space=pltpu.HBM)
     dma = pltpu.SemaphoreType.DMA
     steps_in, steps_out = max(n_in - 1, 1), max(n_out - 1, 1)
-    output, grad_input, weight_grad, bias_grad = pl.pallas_call(
+    scratch = [
+        pltpu.VMEM(features_in.shape, jnp.bfloat16),
+        pltpu.VMEM(upstream.shape, jnp.bfloat16),
+        pltpu.VMEM(kernel_taps.shape, jnp.bfloat16),
+        dma((3,)),
+        pltpu.VMEM((vols, cells // LANES, in_chan * planes, LANES), jnp.float32),
+        pltpu.VMEM((vols, cells // LANES, out_chan * planes, LANES), jnp.float32),
+        pltpu.VMEM((2, vols, in_chan, cells), jnp.bfloat16),
+        pltpu.VMEM((2, vols, out_chan, cells), jnp.bfloat16),
+        pltpu.VMEM((32 * half, LANES), jnp.float32),
+        pltpu.VMEM((out_chan, 27 * in_chan), jnp.bfloat16),
+        pltpu.VMEM((planes * in_chan, (planes + 2) * depth(out_chan)), jnp.bfloat16),
+        pltpu.VMEM((2, vols, in_chan, cells), jnp.bfloat16),
+        pltpu.VMEM((2, vols, out_chan, cells), jnp.bfloat16),
+        pltpu.VMEM((vols, (planes + 2) * 9 * in_chan, cells), jnp.bfloat16),
+        pltpu.VMEM((vols, (planes + 2) * depth(out_chan), cells), jnp.bfloat16),
+        pltpu.VMEM((n_in, n_out * per, LANES), jnp.float32),
+        pltpu.VMEM((steps_in, n_out * per, LANES), jnp.float32),
+        pltpu.VMEM((n_out, per, LANES), jnp.float32),
+        pltpu.VMEM((steps_out, per, LANES), jnp.float32),
+        pltpu.VMEM((n_in, n_out, per, LANES), jnp.bfloat16),
+        pltpu.VMEM((n_in * n_out * per, LANES), jnp.float32),
+        dma((2, 2)),
+        dma((2, 2)),
+        dma((steps_in,)),
+        dma((steps_in,)),
+        dma((steps_out,)),
+        dma((steps_out,)),
+        dma((steps_out,)),
+        dma((steps_out,)),
+        dma((steps_in,)),
+        dma((steps_in,)),
+    ]
+    held = [each for each in scratch if each.memory_space == pltpu.VMEM]
+    grant = sum(math.prod(each.shape) * jnp.dtype(each.dtype).itemsize for each in held)
+    results = pl.pallas_call(
         functools.partial(kernel, sizes, factor),
         out_shape=(
             jax.ShapeDtypeStruct(upstream.shape, jnp.bfloat16),
@@ -342,41 +431,21 @@
             jax.ShapeDtypeStruct(kernel_taps.shape, jnp.float32),
             jax.ShapeDtypeStruct((1, out_chan), jnp.float32),
         ),
-        in_specs=[vmem] * 4,
+        in_specs=[hbm, hbm, hbm, vmem],
         out_specs=(vmem,) * 4,
-        scratch_shapes=[
-            pltpu.VMEM((vols, cells // LANES, in_chan * planes, LANES), jnp.float32),
-            pltpu.VMEM((vols, cells // LANES, out_chan * planes, LANES), jnp.float32),
-            pltpu.VMEM((2, vols, in_chan, cells), jnp.bfloat16),
-            pltpu.VMEM((2, vols, out_chan, cells), jnp.bfloat16),
-            pltpu.VMEM((32 * half, LANES), jnp.float32),
-            pltpu.VMEM((out_chan, 27 * in_chan), jnp.bfloat16),
-            pltpu.VMEM((in_chan, 27 * out_chan), jnp.bfloat16),
-            pltpu.VMEM((2, vols, in_chan, cells), jnp.bfloat16),
-            pltpu.VMEM((2, vols, out_chan, cells), jnp.bfloat16),
-            pltpu.VMEM((vols, (planes + 2) * 9 * in_chan, cells), jnp.bfloat16),
-            pltpu.VMEM((vols, (planes + 2) * 9 * out_chan, cells), jnp.bfloat16),
-            pltpu.VMEM((n_in, n_out * per, LANES), jnp.float32),
-            pltpu.VMEM((steps_in, n_out * per, LANES), jnp.float32),
-            pltpu.VMEM((n_out, per, LANES), jnp.float32),
-            pltpu.VMEM((steps_out, per, LANES), jnp.float32),
-            pltpu.VMEM((n_in, n_out, per, LANES), jnp.bfloat16),
-            pltpu.VMEM((n_in * n_out * per, LANES), jnp.float32),
-            dma((2, 2)),
-            dma((2, 2)),
-            dma((steps_in,)),
-            dma((steps_in,)),
-            dma((steps_out,)),
-            dma((steps_out,)),
-            dma((steps_out,)),
-            dma((steps_out,)),
-            dma((steps_in,)),
-            dma((steps_in,)),
-        ],
+        scratch_shapes=scratch,
         compiler_params=pltpu.CompilerParams(
-            collective_id=0, has_side_effects=True, vmem_limit_bytes=56 * 2**20
+            collective_id=0, has_side_effects=True, vmem_limit_bytes=grant + 6 * 2**20
         ),
     )(features_in, upstream, kernel_taps, channel_bias.reshape(1, out_chan))
+    output, grad_input, weight_grad, bias_grad = pl.pallas_call(
+        finish,
+        out_shape=tuple(jax.ShapeDtypeStruct(each.shape, each.dtype) for each in results),
+        in_specs=[vmem] * 4,
+        out_specs=(hbm,) * 4,
+        scratch_shapes=[dma((4,))],
+        compiler_params=pltpu.CompilerParams(vmem_limit_bytes=4 * 2**20),
+    )(*results)
     return (output, grad_input, weight_grad, bias_grad.reshape(out_chan))
 
 

time: 30.9 us -> 30.1 us (0.974)
  Pallas kernels: 26.5 us -> 25.9 us
    pallas_call x1, Pallas kernels: 26.5 us -> 25 us  [on_device(): pl.pallas_call(functools.partial(kernel, sizes, factor), out_shape=(jax.S...]
    pallas_call x0 -> x1, Pallas kernels: none -> 0.87 us  [on_device(): pl.pallas_call(finish, out_shape=tuple((jax.ShapeDtypeStruct(each.shape,...]
    unnamed x10 -> x8, local copies, waits for them, and re-layouts: 3.67 us -> 3.41 us
where the time goes in v3:
time: 30.1 us; the launch traced here: 29.9 us
  Pallas kernels  25.9 us (86%)
  local copies, waits for them, and re-layouts  3.41 us (11%)
  between operations  0.65 us (2%)
    pallas_call x1, Pallas kernels, on_device(): pl.pallas_call(functools.partial(kernel, sizes, factor), out_shape=(jax.S...  25 us
    unnamed x8, local copies, waits for them, and re-layouts  3.41 us
    pallas_call x1, Pallas kernels, on_device(): pl.pallas_call(finish, out_shape=tuple((jax.ShapeDtypeStruct(each.shape,...  0.87 us

profile of v3, /device:TPU:0, one launch (start us, length us, event | category | flops | bytes accessed | tf_op | source)
XLA Modules:
  0.0 29.9 jit_solution(6030074839566687635)
XLA Ops:
  0.6 0.0 copy-start.3
  0.6 0.6 %copy-done.3 = f32[64]{0:T(128)S(1)} copy-done((f32[64]{0:T(128)S(1)}, f32[64]{0:T(128)}, u32[]{:S(2)}) %copy-start.3) | copy-done | bytes 280
  1.3 0.0 copy-start
  1.3 0.9 %copy-done = bf16[1,64,4,512]{3,2,1,0:T(4,128)(2,1)S(1)} copy-done((bf16[1,64,4,512]{3,2,1,0:T(4,128)(2,1)S(1)}, bf16[1,64,4,512]{3,2,1,0:T(4,128)(2,1)}, u32[]{:S(2)}) %copy-start) | copy-done | bytes 262168
  2.2 0.0 copy-start.1
  2.2 0.9 %copy-done.1 = bf16[1,32,4,512]{3,2,1,0:T(4,128)(2,1)S(1)} copy-done((bf16[1,32,4,512]{3,2,1,0:T(4,128)(2,1)S(1)}, bf16[1,32,4,512]{3,2,1,0:T(4,128)(2,1)}, u32[]{:S(2)}) %copy-start.1) | copy-done | bytes 131096
  3.1 0.0 copy-start.2
  3.1 0.9 %copy-done.2 = bf16[27,2048]{1,0:T(8,128)(2,1)S(1)} copy-done((bf16[27,2048]{1,0:T(8,128)(2,1)S(1)}, bf16[27,2048]{1,0:T(8,128)(2,1)}, u32[]{:S(2)}) %copy-start.2) | copy-done | bytes 110616
  4.0 25.0 %shard_map.75 = (bf16[1,64,4,512]{3,2,1,0:T(4,128)(2,1)S(1)}, bf16[1,32,4,512]{3,2,1,0:T(4,128)(2,1)S(1)}, f32[27,2048]{1,0:T(8,128)S(1)}, f32[1,64]{1,0:T(1,128)S(1)}) custom-call(bf16[1,32,4,512]{3,2,1,0:T(4,128)(2,1)S(1)} %copy-done.1, bf16[1,64,4,512]{3,2,1,0:T(4,128)(2,1)S(1)} %copy-done, bf16[27,2048]{1,0:T(8,128)(2,1)S(1)} %copy-done.2, ...), custom_call_target="tpu_custom_call" | custom-call | tf_op jit(solution)/shard_map/pallas_call | solution.py:426
  29.1 0.9 %shard_map.76 = (bf16[1,64,4,512]{3,2,1,0:T(4,128)(2,1)}, bf16[1,32,4,512]{3,2,1,0:T(4,128)(2,1)}, f32[27,2048]{1,0:T(8,128)}, f32[1,64]{1,0:T(1,128)}) custom-call(bf16[1,64,4,512]{3,2,1,0:T(4,128)(2,1)S(1)} %get-tuple-element.12.refs_0_, bf16[1,32,4,512]{3,2,1,0:T(4,128)(2,1)S(1)} %get-tuple-element.13.refs_1_, f32[27,2048]{1,0:T(8,128)S(1)} %get-tuple-element.14.refs_2_, ...), custom_call_target="tpu_custom_call" | custom-call | tf_op jit(solution)/shard_map/pallas_call | solution.py:441
Async XLA Ops:
  0.6 0.7 %copy-start.3 = (f32[64]{0:T(128)S(1)}, f32[64]{0:T(128)}, u32[]{:S(2)}) copy-start(f32[64]{0:T(128)} %param.6) | copy-start | bytes 772
  1.3 0.9 %copy-start = (bf16[1,64,4,512]{3,2,1,0:T(4,128)(2,1)S(1)}, bf16[1,64,4,512]{3,2,1,0:T(4,128)(2,1)}, u32[]{:S(2)}) copy-start(bf16[1,64,4,512]{3,2,1,0:T(4,128)(2,1)} %u_hbm.1) | copy-start | bytes 786436
  2.2 0.9 %copy-start.1 = (bf16[1,32,4,512]{3,2,1,0:T(4,128)(2,1)S(1)}, bf16[1,32,4,512]{3,2,1,0:T(4,128)(2,1)}, u32[]{:S(2)}) copy-start(bf16[1,32,4,512]{3,2,1,0:T(4,128)(2,1)} %x_hbm.1) | copy-start | bytes 393220
  3.1 0.9 %copy-start.2 = (bf16[27,2048]{1,0:T(8,128)(2,1)S(1)}, bf16[27,2048]{1,0:T(8,128)(2,1)}, u32[]{:S(2)}) copy-start(bf16[27,2048]{1,0:T(8,128)(2,1)} %taps_hbm.1) | copy-start | bytes 331780

commit v4 on v3

--- a/solution.py
+++ b/solution.py
@@ -41,9 +41,10 @@
 
 
 def kernel(
-    sizes, factor, x_hbm, u_hbm, taps_hbm, bias_ref, out_ref, gi_ref, wg_ref, bg_ref,
-    x_ref, u_ref, taps_ref, load, rows_x, rows_u, edge_x, edge_u, taps_rows, wf, wb,
-    halo_x, halo_u, near_x, near_u, part, recv_in, acc, recv_out, gath, sums,
+    sizes, factor, x_hbm, u_hbm, taps_hbm, bias_hbm, out_ref, gi_ref, wg_ref, bg_ref,
+    x_ref, u_ref, taps_ref, bias_ref, load, grads, rows_x, rows_u, edge_x, edge_u, taps_rows, wf, wb,
+    halo_x, halo_u, near_x, near_u, part_a, part_b, recv_a, recv_b, acc, recv_out, gath,
+    sums_a, sums_b,
     halo_send, halo_recv, in_send, in_recv, out_send, out_recv,
     gout_send, gout_recv, gin_send, gin_recv,
 ):
@@ -90,9 +91,10 @@
             value = jnp.concatenate([rows[vol, tile, at, :] for tile in range(tiles)], axis=1)
             ref[vol, i] = value.astype(jnp.bfloat16)
 
+    moves = ((x_hbm, x_ref), (u_hbm, u_ref), (taps_hbm, taps_ref), (bias_hbm, bias_ref))
     loads = [
         pltpu.make_async_copy(source, target, load.at[at])
-        for at, (source, target) in enumerate(((x_hbm, x_ref), (u_hbm, u_ref), (taps_hbm, taps_ref)))
+        for at, (source, target) in enumerate(moves)
     ]
     for copy in loads:
         copy.start()
@@ -137,9 +139,6 @@
             def _(side=side):
                 halo_copies(side, (which,))[0].start()
 
-    def center(slot):
-        return slot * deep_u + 4 * out_chan
-
     send_halos(0)
     loads[1].wait()
     for vol in range(vols):
@@ -147,9 +146,9 @@
         for z in range(planes):
             for piece in range(out_chan // ROWS):
                 value = piece_u(vol, z, piece).astype(jnp.bfloat16)
-                near_u[vol, pl.ds(center(z + 1) + piece * ROWS, ROWS), :] = value
+                grads[vol, pl.ds(z * out_chan + piece * ROWS, ROWS), :] = value
         for side, z in ((0, planes - 1), (1, 0)):
-            edge_u[side, vol] = near_u[vol, pl.ds(center(z + 1), out_chan), :]
+            edge_u[side, vol] = grads[vol, pl.ds(z * out_chan, out_chan), :]
     send_halos(1)
     lanes = (((1,), (1,)), ((), ()))
     for vol in range(vols):
@@ -157,25 +156,62 @@
             for piece in range(2):
                 fill(near_x, vol, (z + 1) * deep_x, in_chan, piece, piece_x(vol, z, piece))
 
+    def product(vol, slot, count, at, wide):
+        window = near_x[vol, pl.ds(slot * deep_x, count * deep_x), :]
+        grad = grads[vol, pl.ds(at, wide), :]
+        return lax.dot_general(window, grad, lanes, preferred_element_type=jnp.float32)
+
+    def lane_tile(value, k):
+        return value[:, k * LANES : (k + 1) * LANES]
+
+    last = planes * out_chan - LANES
+    even = [jnp.zeros((deep_x, LANES), jnp.float32) for _ in range(3)]
+    odd = [jnp.zeros((deep_x, LANES), jnp.float32) for _ in range(3)]
     ones = jnp.ones((8, cells), jnp.bfloat16)
-    bias_term = jnp.zeros((8, out_chan), jnp.float32)
-    terms = [jnp.zeros((deep_x, out_chan), jnp.float32) for _ in range(3)]
-
-    def grad(vol, z):
-        return near_u[vol, pl.ds(center(z + 1), out_chan), :]
-
-    def pair(vol, z, tap):
-        window = near_x[vol, pl.ds((z + tap) * deep_x, deep_x), :]
-        return lax.dot_general(window, grad(vol, z), lanes, preferred_element_type=jnp.float32)
-
-    for vol in range(vols):
-        for z in range(planes):
-            bias_term += lax.dot_general(
-                ones, grad(vol, z), lanes, preferred_element_type=jnp.float32
-            )
-            for tap in range(3):
+    bias_term = jnp.zeros((8, LANES), jnp.float32)
+    for vol in range(vols):
+        inside = product(vol, 1, planes, 0, planes * out_chan)
+        for tap in range(3):
+            for z in range(planes):
                 if 1 <= z + tap <= planes:
-                    terms[tap] += pair(vol, z, tap)
+                    low = (z + tap - 1) * deep_x
+                    kept = odd if z % 2 else even
+                    kept[tap] += lane_tile(inside[low : low + deep_x], z // 2)
+        bias_all = lax.dot_general(
+            ones, grads[vol], lanes, preferred_element_type=jnp.float32
+        )
+        for k in range(planes // 2):
+            bias_term += lane_tile(bias_all, k)
+
+    def packed(tap):
+        first = even[tap].reshape(9, 2, half, LANES)
+        second = odd[tap].reshape(9, 2, half, LANES)
+        low = lax.broadcasted_iota(jnp.int32, (9, half, LANES), 2) < out_chan
+        stay = jnp.where(low, first[:, 0], second[:, 1]).reshape(9 * half, LANES)
+        move = jnp.where(low, first[:, 1], second[:, 0]).reshape(9 * half, LANES)
+        return stay + pltpu.roll(move, out_chan, 1)
+
+    def lay(part, pieces):
+        rest = math.prod(part.shape[:2]) - sum(each.shape[0] for each in pieces)
+        if rest:
+            pieces = pieces + [jnp.zeros((rest, LANES), jnp.float32)]
+        part[...] = jnp.concatenate(pieces, axis=0).reshape(part.shape)
+
+    def in_copy(step, second):
+        peer, device = inner_peer(step)
+        return pltpu.make_async_remote_copy(
+            src_ref=(part_b if second else part_a).at[peer],
+            dst_ref=(recv_b if second else recv_a).at[step - 1],
+            send_sem=in_send.at[second, step - 1],
+            recv_sem=in_recv.at[second, step - 1],
+            device_id=device,
+            device_id_type=MESH,
+        )
+
+    bias_term += pltpu.roll(bias_term, out_chan, 1)
+    lay(part_a, [packed(1), bias_term])
+    for step in range(1, n_in):
+        in_copy(step, 0).start()
 
     for side in range(2):
 
@@ -193,29 +229,11 @@
             for piece in range(2):
                 field = halo_x[side, vol, pl.ds(piece * half, half), :].astype(jnp.float32)
                 fill(near_x, vol, slot * deep_x, in_chan, piece, field)
-        terms[0] += pair(vol, 0, 0)
-        terms[2] += pair(vol, planes - 1, 2)
-    term = jnp.concatenate(terms, axis=0)
-    term = term.reshape(27, 2, half, out_chan)
-    term = jnp.concatenate([term[:, 0], term[:, 1]], axis=-1).reshape(27 * half, 2 * out_chan)
-    bias_term = jnp.concatenate([bias_term, jnp.zeros_like(bias_term)], axis=-1)
-    chunk = part.shape[1]
-    filled = 27 * half + 8
-    whole = jnp.concatenate(
-        [term, bias_term, jnp.zeros((n_in * chunk - filled, LANES), jnp.float32)], axis=0
-    )
-    part[...] = whole.reshape(part.shape)
-
-    def in_copy(step):
-        peer, device = inner_peer(step)
-        return pltpu.make_async_remote_copy(
-            src_ref=part.at[peer],
-            dst_ref=recv_in.at[step - 1],
-            send_sem=in_send.at[step - 1],
-            recv_sem=in_recv.at[step - 1],
-            device_id=device,
-            device_id_type=MESH,
-        )
+        even[0] += product(vol, 0, 1, 0, LANES)
+        odd[2] += product(vol, planes + 1, 1, last, LANES)
+    lay(part_b, [packed(0), packed(2)])
+    for step in range(1, n_in):
+        in_copy(step, 1).start()
 
     def out_copy(step):
         peer, device = outer_peer(step)
@@ -248,10 +266,8 @@
             device_id_type=MESH,
         )
 
-    for step in range(1, n_in):
-        in_copy(step).start()
-
     loads[2].wait()
+    loads[3].wait()
     stride = taps_rows.shape[0] // half
     for j in range(half):
         taps_rows[pl.ds(j * stride, 27), :] = taps_ref[:, pl.ds(j * LANES, LANES)].astype(jnp.float32)
@@ -292,11 +308,13 @@
             value = lax.dot_general(wf[...], window, rows, preferred_element_type=jnp.float32)
             put(rows_u, vol, pl.ds(z, out_chan, stride=planes), value + bias)
     for step in range(1, n_in):
-        in_copy(step).wait_recv()
-    total = part[me_in]
-    for step in range(1, n_in):
-        total += recv_in[step - 1]
-    acc[...] = total.reshape(acc.shape)
+        in_copy(step, 0).wait_recv()
+        in_copy(step, 1).wait_recv()
+    total_a, total_b = part_a[me_in], part_b[me_in]
+    for step in range(1, n_in):
+        total_a += recv_a[step - 1]
+        total_b += recv_b[step - 1]
+    acc[...] = jnp.concatenate([total_a, total_b], axis=0).reshape(acc.shape)
     for step in range(1, n_out):
         out_copy(step).start()
 
@@ -346,10 +364,19 @@
         unite(rows_x, vol, gi_ref, in_chan)
     for step in range(1, n_in):
         gather_in_copy(step).wait_recv()
-    sums[...] = gath[...].astype(jnp.float32).reshape(sums.shape)
+    size_a, size_b = part_a.shape[1], part_b.shape[1]
+    for peer in range(n_in):
+        value = gath[peer].astype(jnp.float32).reshape(size_a + size_b, LANES)
+        sums_a[pl.ds(peer * size_a, size_a), :] = value[:size_a]
+        sums_b[pl.ds(peer * size_b, size_b), :] = value[size_a:]
     for j in range(half):
-        wg_ref[:, pl.ds(j * LANES, LANES)] = sums[pl.ds(j, 27, stride=half), :]
-    bg_ref[...] = sums[pl.ds(27 * half, 1), :out_chan]
+        value = [
+            sums_b[pl.ds(j, 9, stride=half), :],
+            sums_a[pl.ds(j, 9, stride=half), :],
+            sums_b[pl.ds(9 * half + j, 9, stride=half), :],
+        ]
+        wg_ref[:, pl.ds(j * LANES, LANES)] = jnp.concatenate(value, axis=0)
+    bg_ref[...] = sums_a[pl.ds(9 * half, 1), :out_chan]
 
     for side in range(2):
 
@@ -359,7 +386,8 @@
                 copy.wait_send()
 
     for step in range(1, n_in):
-        in_copy(step).wait_send()
+        in_copy(step, 0).wait_send()
+        in_copy(step, 1).wait_send()
         gather_in_copy(step).wait_send()
     for step in range(1, n_out):
         out_copy(step).wait_send()
@@ -382,8 +410,10 @@
     half = in_chan // 2
     cells_all = vols * inner_dp * n_out * planes * n_gz * cells
     factor = 1.0 / math.sqrt(cells_all)
-    filled = 27 * half + 8
-    per = ROWS * -(-filled // (ROWS * n_in * n_out))
+    size_a = 8 * -(-(9 * half + 8) // (8 * n_in))
+    size_b = 8 * -(-(18 * half) // (8 * n_in))
+    per = ROWS * -(-(size_a + size_b) // (ROWS * n_out))
+    size_b = n_out * per - size_a
     vmem = pl.BlockSpec(memory_space=pltpu.VMEM)
     hbm = pl.BlockSpec(memory_space=pltpu.HBM)
     dma = pltpu.SemaphoreType.DMA
@@ -392,7 +422,9 @@
         pltpu.VMEM(features_in.shape, jnp.bfloat16),
         pltpu.VMEM(upstream.shape, jnp.bfloat16),
         pltpu.VMEM(kernel_taps.shape, jnp.bfloat16),
-        dma((3,)),
+        pltpu.VMEM((1, out_chan), jnp.float32),
+        dma((4,)),
+        pltpu.VMEM((vols, planes * out_chan, cells), jnp.bfloat16),
         pltpu.VMEM((vols, cells // LANES, in_chan * planes, LANES), jnp.float32),
         pltpu.VMEM((vols, cells // LANES, out_chan * planes, LANES), jnp.float32),
         pltpu.VMEM((2, vols, in_chan, cells), jnp.bfloat16),
@@ -404,16 +436,19 @@
         pltpu.VMEM((2, vols, out_chan, cells), jnp.bfloat16),
         pltpu.VMEM((vols, (planes + 2) * 9 * in_chan, cells), jnp.bfloat16),
         pltpu.VMEM((vols, (planes + 2) * depth(out_chan), cells), jnp.bfloat16),
-        pltpu.VMEM((n_in, n_out * per, LANES), jnp.float32),
-        pltpu.VMEM((steps_in, n_out * per, LANES), jnp.float32),
+        pltpu.VMEM((n_in, size_a, LANES), jnp.float32),
+        pltpu.VMEM((n_in, size_b, LANES), jnp.float32),
+        pltpu.VMEM((steps_in, size_a, LANES), jnp.float32),
+        pltpu.VMEM((steps_in, size_b, LANES), jnp.float32),
         pltpu.VMEM((n_out, per, LANES), jnp.float32),
         pltpu.VMEM((steps_out, per, LANES), jnp.float32),
         pltpu.VMEM((n_in, n_out, per, LANES), jnp.bfloat16),
-        pltpu.VMEM((n_in * n_out * per, LANES), jnp.float32),
+        pltpu.VMEM((n_in * size_a, LANES), jnp.float32),
+        pltpu.VMEM((n_in * size_b, LANES), jnp.float32),
         dma((2, 2)),
         dma((2, 2)),
-        dma((steps_in,)),
-        dma((steps_in,)),
+        dma((2, steps_in)),
+        dma((2, steps_in)),
         dma((steps_out,)),
         dma((steps_out,)),
         dma((steps_out,)),
@@ -431,13 +466,18 @@
             jax.ShapeDtypeStruct(kernel_taps.shape, jnp.float32),
             jax.ShapeDtypeStruct((1, out_chan), jnp.float32),
         ),
-        in_specs=[hbm, hbm, hbm, vmem],
+        in_specs=[hbm] * 4,
         out_specs=(vmem,) * 4,
         scratch_shapes=scratch,
         compiler_params=pltpu.CompilerParams(
             collective_id=0, has_side_effects=True, vmem_limit_bytes=grant + 6 * 2**20
         ),
-    )(features_in, upstream, kernel_taps, channel_bias.reshape(1, out_chan))
+    )(
+        pltpu.with_memory_space_constraint(features_in, pltpu.HBM),
+        pltpu.with_memory_space_constraint(upstream, pltpu.HBM),
+        pltpu.with_memory_space_constraint(kernel_taps, pltpu.HBM),
+        pltpu.with_memory_space_constraint(channel_bias.reshape(1, out_chan), pltpu.HBM),
+    )
     output, grad_input, weight_grad, bias_grad = pl.pallas_call(
         finish,
         out_shape=tuple(jax.ShapeDtypeStruct(each.shape, each.dtype) for each in results),

time: 30.1 us -> 26.6 us (0.88)
  local copies, waits for them, and re-layouts: 3.41 us -> 0 us
    unnamed x8 -> x0, local copies, waits for them, and re-layouts: 3.41 us -> none
where the time goes in v4:
time: 26.6 us; the launch traced here: 26.5 us
  Pallas kernels  25.8 us (97%)
  between operations  0.64 us (2%)
    pallas_call x1, Pallas kernels, on_device(): pl.pallas_call(functools.partial(kernel, sizes, factor), out_shape=(jax.S...  25 us
    pallas_call x1, Pallas kernels, on_device(): pl.pallas_call(finish, out_shape=tuple((jax.ShapeDtypeStruct(each.shape,...  0.87 us

profile of v4, /device:TPU:0, one launch (start us, length us, event | category | flops | bytes accessed | tf_op | source)
XLA Modules:
  0.0 26.5 jit_solution(381679534745621818)
XLA Ops:
  0.6 25.0 %shard_map.75 = (bf16[1,64,4,512]{3,2,1,0:T(4,128)(2,1)S(1)}, bf16[1,32,4,512]{3,2,1,0:T(4,128)(2,1)S(1)}, f32[27,2048]{1,0:T(8,128)S(1)}, f32[1,64]{1,0:T(1,128)S(1)}) custom-call(bf16[1,32,4,512]{3,2,1,0:T(4,128)(2,1)} %x_hbm.1, bf16[1,64,4,512]{3,2,1,0:T(4,128)(2,1)} %u_hbm.1, bf16[27,2048]{1,0:T(8,128)(2,1)} %taps_hbm.1, f32[1,64]{1,0:T(1,128)} %bitcast.2), custom_call_target="tpu_custom_call" | custom-call | tf_op jit(solution)/shard_map/pallas_call | solution.py:461
  25.6 0.9 %shard_map.76 = (bf16[1,64,4,512]{3,2,1,0:T(4,128)(2,1)}, bf16[1,32,4,512]{3,2,1,0:T(4,128)(2,1)}, f32[27,2048]{1,0:T(8,128)}, f32[1,64]{1,0:T(1,128)}) custom-call(bf16[1,64,4,512]{3,2,1,0:T(4,128)(2,1)S(1)} %get-tuple-element.12.refs_0_, bf16[1,32,4,512]{3,2,1,0:T(4,128)(2,1)S(1)} %get-tuple-element.13.refs_1_, f32[27,2048]{1,0:T(8,128)S(1)} %get-tuple-element.14.refs_2_, ...), custom_call_target="tpu_custom_call" | custom-call | tf_op jit(solution)/shard_map/pallas_call | solution.py:481

commit v5 on v4

--- a/solution.py
+++ b/solution.py
@@ -56,10 +56,12 @@
     me_in = lax.rem(dp, inner_dp) * n_gz + gz
     me_out = lax.div(dp, inner_dp)
 
+    @functools.cache
     def inner_peer(step):
         peer = lax.rem(me_in + step, n_in)
         return peer, {"dp": me_out * inner_dp + lax.div(peer, n_gz), "gz": lax.rem(peer, n_gz)}
 
+    @functools.cache
     def outer_peer(step):
         peer = lax.rem(me_out + step, n_out)
         return peer, {"dp": peer * inner_dp + lax.rem(dp, inner_dp), "gz": gz}
@@ -105,6 +107,13 @@
         pl.semaphore_signal(barrier, inc=1, device_id=outer_peer(step)[1], device_id_type=MESH)
 
     deep_x, deep_u = 9 * in_chan, depth(out_chan)
+    pad = deep_u - 9 * out_chan
+    wb[...] = jnp.zeros_like(wb)
+    for vol in range(vols):
+        if pad:
+            for slot in range(planes + 2):
+                at = pl.ds(slot * deep_u + 9 * out_chan, pad)
+                near_u[vol, at, :] = jnp.zeros((pad, cells), jnp.bfloat16)
     loads[0].wait()
     for vol in range(vols):
         spread(rows_x, vol, x_ref, in_chan)
@@ -280,7 +289,6 @@
     for t in range(0, 27, group):
         some = jnp.concatenate([tap_kernel(t + k) for k in range(min(group, 27 - t))], axis=0)
         wf[:, pl.ds(t * in_chan, some.shape[0])] = some.T.astype(jnp.bfloat16)
-    wb[...] = jnp.zeros_like(wb)
     for a in range(3):
         for t in range(0, 9, 2):
             some = [tap_kernel(26 - 9 * a - t - k) for k in range(min(2, 9 - t))]
@@ -289,17 +297,23 @@
                 at = pl.ds((z + a) * deep_u + t * out_chan, some.shape[1])
                 wb[pl.ds(z * in_chan, in_chan), at] = some
 
-    pad = deep_u - 9 * out_chan
-    for vol in range(vols):
-        if pad:
-            for slot in range(planes + 2):
-                at = pl.ds(slot * deep_u + 9 * out_chan, pad)
-                near_u[vol, at, :] = jnp.zeros((pad, cells), jnp.bfloat16)
+    for vol in range(vols):
         for z in range(planes):
             for piece in range(out_chan // ROWS):
                 fill(near_u, vol, (z + 1) * deep_u, out_chan, piece, piece_u(vol, z, piece))
 
     rows = (((1,), (0,)), ((), ()))
+    for step in range(1, n_in):
+        in_copy(step, 0).wait_recv()
+        in_copy(step, 1).wait_recv()
+    total_a, total_b = part_a[me_in], part_b[me_in]
+    for step in range(1, n_in):
+        total_a += recv_a[step - 1]
+        total_b += recv_b[step - 1]
+    acc[...] = jnp.concatenate([total_a, total_b], axis=0).reshape(acc.shape)
+    for step in range(1, n_out):
+        out_copy(step).start()
+
     bias = jnp.broadcast_to(bias_ref[...], (LANES, out_chan)).T
     bias = jnp.concatenate([bias] * (cells // LANES), axis=1)
     for vol in range(vols):
@@ -307,31 +321,6 @@
             window = near_x[vol, pl.ds(z * deep_x, 3 * deep_x), :]
             value = lax.dot_general(wf[...], window, rows, preferred_element_type=jnp.float32)
             put(rows_u, vol, pl.ds(z, out_chan, stride=planes), value + bias)
-    for step in range(1, n_in):
-        in_copy(step, 0).wait_recv()
-        in_copy(step, 1).wait_recv()
-    total_a, total_b = part_a[me_in], part_b[me_in]
-    for step in range(1, n_in):
-        total_a += recv_a[step - 1]
-        total_b += recv_b[step - 1]
-    acc[...] = jnp.concatenate([total_a, total_b], axis=0).reshape(acc.shape)
-    for step in range(1, n_out):
-        out_copy(step).start()
-
-    for side in range(2):
-
-        @pl.when(gets[side])
-        def _(side=side):
-            halo_copies(side, (1,))[0].wait_recv()
-
-    for vol in range(vols):
-        for side, slot in ((0, 0), (1, planes + 1)):
-            for piece in range(out_chan // ROWS):
-                field = halo_u[side, vol, pl.ds(piece * ROWS, ROWS), :].astype(jnp.float32)
-                fill(near_u, vol, slot * deep_u, out_chan, piece, field)
-    for vol in range(vols):
-        unite(rows_u, vol, out_ref, out_chan)
-
     def backward(first):
         tile = min(2 * LANES, cells)
         for vol in range(vols):
@@ -354,11 +343,24 @@
     gath[me_in, me_out] = (total * factor).astype(jnp.bfloat16)
     for step in range(1, n_out):
         gather_out_copy(step).start()
+    for side in range(2):
+
+        @pl.when(gets[side])
+        def _(side=side):
+            halo_copies(side, (1,))[0].wait_recv()
+
+    for vol in range(vols):
+        for side, slot in ((0, 0), (1, planes + 1)):
+            for piece in range(out_chan // ROWS):
+                field = halo_u[side, vol, pl.ds(piece * ROWS, ROWS), :].astype(jnp.float32)
+                fill(near_u, vol, slot * deep_u, out_chan, piece, field)
     backward(True)
     for step in range(1, n_out):
         gather_out_copy(step).wait_recv()
     for step in range(1, n_in):
         gather_in_copy(step).start()
+    for vol in range(vols):
+        unite(rows_u, vol, out_ref, out_chan)
     backward(False)
     for vol in range(vols):
         unite(rows_x, vol, gi_ref, in_chan)

time: 26.6 us -> 26.6 us (level)
  no operation moved by 1% of the time
where the time goes in v5:
time: 26.6 us; the launch traced here: 26.5 us
  Pallas kernels  25.8 us (97%)
  between operations  0.64 us (2%)
    pallas_call x1, Pallas kernels, on_device(): pl.pallas_call(functools.partial(kernel, sizes, factor), out_shape=(jax.S...  25 us
    pallas_call x1, Pallas kernels, on_device(): pl.pallas_call(finish, out_shape=tuple((jax.ShapeDtypeStruct(each.shape,...  0.87 us

profile of v5, /device:TPU:0, one launch (start us, length us, event | category | flops | bytes accessed | tf_op | source)
XLA Modules:
  0.0 26.5 jit_solution(16250718218593807064)
XLA Ops:
  0.6 25.0 %shard_map.75 = (bf16[1,64,4,512]{3,2,1,0:T(4,128)(2,1)S(1)}, bf16[1,32,4,512]{3,2,1,0:T(4,128)(2,1)S(1)}, f32[27,2048]{1,0:T(8,128)S(1)}, f32[1,64]{1,0:T(1,128)S(1)}) custom-call(bf16[1,32,4,512]{3,2,1,0:T(4,128)(2,1)} %x_hbm.1, bf16[1,64,4,512]{3,2,1,0:T(4,128)(2,1)} %u_hbm.1, bf16[27,2048]{1,0:T(8,128)(2,1)} %taps_hbm.1, f32[1,64]{1,0:T(1,128)} %bitcast.2), custom_call_target="tpu_custom_call" | custom-call | tf_op jit(solution)/shard_map/pallas_call | solution.py:463
  25.6 0.9 %shard_map.76 = (bf16[1,64,4,512]{3,2,1,0:T(4,128)(2,1)}, bf16[1,32,4,512]{3,2,1,0:T(4,128)(2,1)}, f32[27,2048]{1,0:T(8,128)}, f32[1,64]{1,0:T(1,128)}) custom-call(bf16[1,64,4,512]{3,2,1,0:T(4,128)(2,1)S(1)} %get-tuple-element.12.refs_0_, bf16[1,32,4,512]{3,2,1,0:T(4,128)(2,1)S(1)} %get-tuple-element.13.refs_1_, f32[27,2048]{1,0:T(8,128)S(1)} %get-tuple-element.14.refs_2_, ...), custom_call_target="tpu_custom_call" | custom-call | tf_op jit(solution)/shard_map/pallas_call | solution.py:483

commit v6 on v5

--- a/solution.py
+++ b/solution.py
@@ -106,14 +106,16 @@
     for step in range(1, n_out):
         pl.semaphore_signal(barrier, inc=1, device_id=outer_peer(step)[1], device_id_type=MESH)
 
-    deep_x, deep_u = 9 * in_chan, depth(out_chan)
-    pad = deep_u - 9 * out_chan
+    deep_x, deep_u = depth(in_chan), depth(out_chan)
     wb[...] = jnp.zeros_like(wb)
-    for vol in range(vols):
-        if pad:
-            for slot in range(planes + 2):
-                at = pl.ds(slot * deep_u + 9 * out_chan, pad)
-                near_u[vol, at, :] = jnp.zeros((pad, cells), jnp.bfloat16)
+    wf[...] = jnp.zeros_like(wf)
+    for vol in range(vols):
+        for near, deep, chan in ((near_x, deep_x, in_chan), (near_u, deep_u, out_chan)):
+            pad = deep - 9 * chan
+            if pad:
+                for slot in range(planes + 2):
+                    at = pl.ds(slot * deep + 9 * chan, pad)
+                    near[vol, at, :] = jnp.zeros((pad, cells), jnp.bfloat16)
     loads[0].wait()
     for vol in range(vols):
         spread(rows_x, vol, x_ref, in_chan)
@@ -165,8 +167,8 @@
             for piece in range(2):
                 fill(near_x, vol, (z + 1) * deep_x, in_chan, piece, piece_x(vol, z, piece))
 
-    def product(vol, slot, count, at, wide):
-        window = near_x[vol, pl.ds(slot * deep_x, count * deep_x), :]
+    def product(vol, slot, at, wide):
+        window = near_x[vol, pl.ds(slot * deep_x, 9 * in_chan), :]
         grad = grads[vol, pl.ds(at, wide), :]
         return lax.dot_general(window, grad, lanes, preferred_element_type=jnp.float32)
 
@@ -174,18 +176,18 @@
         return value[:, k * LANES : (k + 1) * LANES]
 
     last = planes * out_chan - LANES
-    even = [jnp.zeros((deep_x, LANES), jnp.float32) for _ in range(3)]
-    odd = [jnp.zeros((deep_x, LANES), jnp.float32) for _ in range(3)]
+    even = [jnp.zeros((9 * in_chan, LANES), jnp.float32) for _ in range(3)]
+    odd = [jnp.zeros((9 * in_chan, LANES), jnp.float32) for _ in range(3)]
     ones = jnp.ones((8, cells), jnp.bfloat16)
     bias_term = jnp.zeros((8, LANES), jnp.float32)
     for vol in range(vols):
-        inside = product(vol, 1, planes, 0, planes * out_chan)
-        for tap in range(3):
-            for z in range(planes):
-                if 1 <= z + tap <= planes:
-                    low = (z + tap - 1) * deep_x
+        for slot in range(1, planes + 1):
+            inside = product(vol, slot, 0, planes * out_chan)
+            for tap in range(3):
+                z = slot - tap
+                if 0 <= z < planes:
                     kept = odd if z % 2 else even
-                    kept[tap] += lane_tile(inside[low : low + deep_x], z // 2)
+                    kept[tap] += lane_tile(inside, z // 2)
         bias_all = lax.dot_general(
             ones, grads[vol], lanes, preferred_element_type=jnp.float32
         )
@@ -238,8 +240,8 @@
             for piece in range(2):
                 field = halo_x[side, vol, pl.ds(piece * half, half), :].astype(jnp.float32)
                 fill(near_x, vol, slot * deep_x, in_chan, piece, field)
-        even[0] += product(vol, 0, 1, 0, LANES)
-        odd[2] += product(vol, planes + 1, 1, last, LANES)
+        even[0] += product(vol, 0, 0, LANES)
+        odd[2] += product(vol, planes + 1, last, LANES)
     lay(part_b, [packed(0), packed(2)])
     for step in range(1, n_in):
         in_copy(step, 1).start()
@@ -286,9 +288,13 @@
         return jnp.concatenate([both[:, :out_chan], both[:, out_chan:]], axis=0)
 
     group = LANES // in_chan
-    for t in range(0, 27, group):
-        some = jnp.concatenate([tap_kernel(t + k) for k in range(min(group, 27 - t))], axis=0)
-        wf[:, pl.ds(t * in_chan, some.shape[0])] = some.T.astype(jnp.bfloat16)
+    for a in range(3):
+        for t in range(0, 9, group):
+            some = [tap_kernel(9 * a + t + k) for k in range(min(group, 9 - t))]
+            some = jnp.concatenate(some, axis=0).T.astype(jnp.bfloat16)
+            for z in range(planes):
+                at = pl.ds((z + a) * deep_x + t * in_chan, some.shape[1])
+                wf[pl.ds(z * out_chan, out_chan), at] = some
     for a in range(3):
         for t in range(0, 9, 2):
             some = [tap_kernel(26 - 9 * a - t - k) for k in range(min(2, 9 - t))]
@@ -317,10 +323,11 @@
     bias = jnp.broadcast_to(bias_ref[...], (LANES, out_chan)).T
     bias = jnp.concatenate([bias] * (cells // LANES), axis=1)
     for vol in range(vols):
+        value = lax.dot_general(wf[...], near_x[vol], rows, preferred_element_type=jnp.float32)
         for z in range(planes):
-            window = near_x[vol, pl.ds(z * deep_x, 3 * deep_x), :]
-            value = lax.dot_general(wf[...], window, rows, preferred_element_type=jnp.float32)
-            put(rows_u, vol, pl.ds(z, out_chan, stride=planes), value + bias)
+            plane = value[z * out_chan : (z + 1) * out_chan]
+            put(rows_u, vol, pl.ds(z, out_chan, stride=planes), plane + bias)
+
     def backward(first):
         tile = min(2 * LANES, cells)
         for vol in range(vols):
@@ -432,11 +439,11 @@
         pltpu.VMEM((2, vols, in_chan, cells), jnp.bfloat16),
         pltpu.VMEM((2, vols, out_chan, cells), jnp.bfloat16),
         pltpu.VMEM((32 * half, LANES), jnp.float32),
-        pltpu.VMEM((out_chan, 27 * in_chan), jnp.bfloat16),
+        pltpu.VMEM((planes * out_chan, (planes + 2) * depth(in_chan)), jnp.bfloat16),
         pltpu.VMEM((planes * in_chan, (planes + 2) * depth(out_chan)), jnp.bfloat16),
         pltpu.VMEM((2, vols, in_chan, cells), jnp.bfloat16),
         pltpu.VMEM((2, vols, out_chan, cells), jnp.bfloat16),
-        pltpu.VMEM((vols, (planes + 2) * 9 * in_chan, cells), jnp.bfloat16),
+        pltpu.VMEM((vols, (planes + 2) * depth(in_chan), cells), jnp.bfloat16),
         pltpu.VMEM((vols, (planes + 2) * depth(out_chan), cells), jnp.bfloat16),
         pltpu.VMEM((n_in, size_a, LANES), jnp.float32),
         pltpu.VMEM((n_in, size_b, LANES), jnp.float32),

time: 26.6 us -> 26.5 us (level)
  no operation moved by 1% of the time
where the time goes in v6:
time: 26.5 us; the launch traced here: 26.4 us
  Pallas kernels  25.7 us (97%)
  between operations  0.64 us (2%)
    pallas_call x1, Pallas kernels, on_device(): pl.pallas_call(functools.partial(kernel, sizes, factor), out_shape=(jax.S...  24.8 us
    pallas_call x1, Pallas kernels, on_device(): pl.pallas_call(finish, out_shape=tuple((jax.ShapeDtypeStruct(each.shape,...  0.87 us

profile of v6, /device:TPU:0, one launch (start us, length us, event | category | flops | bytes accessed | tf_op | source)
XLA Modules:
  0.0 26.4 jit_solution(12875768295841784909)
XLA Ops:
  0.6 24.8 %shard_map.75 = (bf16[1,64,4,512]{3,2,1,0:T(4,128)(2,1)S(1)}, bf16[1,32,4,512]{3,2,1,0:T(4,128)(2,1)S(1)}, f32[27,2048]{1,0:T(8,128)S(1)}, f32[1,64]{1,0:T(1,128)S(1)}) custom-call(bf16[1,32,4,512]{3,2,1,0:T(4,128)(2,1)} %x_hbm.1, bf16[1,64,4,512]{3,2,1,0:T(4,128)(2,1)} %u_hbm.1, bf16[27,2048]{1,0:T(8,128)(2,1)} %taps_hbm.1, f32[1,64]{1,0:T(1,128)} %bitcast.2), custom_call_target="tpu_custom_call" | custom-call | tf_op jit(solution)/shard_map/pallas_call | solution.py:470
  25.5 0.9 %shard_map.76 = (bf16[1,64,4,512]{3,2,1,0:T(4,128)(2,1)}, bf16[1,32,4,512]{3,2,1,0:T(4,128)(2,1)}, f32[27,2048]{1,0:T(8,128)}, f32[1,64]{1,0:T(1,128)}) custom-call(bf16[1,64,4,512]{3,2,1,0:T(4,128)(2,1)S(1)} %get-tuple-element.12.refs_0_, bf16[1,32,4,512]{3,2,1,0:T(4,128)(2,1)S(1)} %get-tuple-element.13.refs_1_, f32[27,2048]{1,0:T(8,128)S(1)} %get-tuple-element.14.refs_2_, ...), custom_call_target="tpu_custom_call" | custom-call | tf_op jit(solution)/shard_map/pallas_call | solution.py:490

commit v7 on v6

--- a/solution.py
+++ b/solution.py
@@ -160,7 +160,6 @@
                 grads[vol, pl.ds(z * out_chan + piece * ROWS, ROWS), :] = value
         for side, z in ((0, planes - 1), (1, 0)):
             edge_u[side, vol] = grads[vol, pl.ds(z * out_chan, out_chan), :]
-    send_halos(1)
     lanes = (((1,), (1,)), ((), ()))
     for vol in range(vols):
         for z in range(planes):
@@ -319,6 +318,7 @@
     acc[...] = jnp.concatenate([total_a, total_b], axis=0).reshape(acc.shape)
     for step in range(1, n_out):
         out_copy(step).start()
+    send_halos(1)
 
     bias = jnp.broadcast_to(bias_ref[...], (LANES, out_chan)).T
     bias = jnp.concatenate([bias] * (cells // LANES), axis=1)

time: 26.5 us -> 26.3 us (level)
  no operation moved by 1% of the time
where the time goes in v7:
time: 26.3 us; the launch traced here: 26.1 us
  Pallas kernels  25.5 us (97%)
  between operations  0.64 us (2%)
    pallas_call x1, Pallas kernels, on_device(): pl.pallas_call(functools.partial(kernel, sizes, factor), out_shape=(jax.S...  24.6 us
    pallas_call x1, Pallas kernels, on_device(): pl.pallas_call(finish, out_shape=tuple((jax.ShapeDtypeStruct(each.shape,...  0.87 us

profile of v7, /device:TPU:0, one launch (start us, length us, event | category | flops | bytes accessed | tf_op | source)
XLA Modules:
  0.0 26.1 jit_solution(9317814795360230337)
XLA Ops:
  0.6 24.6 %shard_map.75 = (bf16[1,64,4,512]{3,2,1,0:T(4,128)(2,1)S(1)}, bf16[1,32,4,512]{3,2,1,0:T(4,128)(2,1)S(1)}, f32[27,2048]{1,0:T(8,128)S(1)}, f32[1,64]{1,0:T(1,128)S(1)}) custom-call(bf16[1,32,4,512]{3,2,1,0:T(4,128)(2,1)} %x_hbm.1, bf16[1,64,4,512]{3,2,1,0:T(4,128)(2,1)} %u_hbm.1, bf16[27,2048]{1,0:T(8,128)(2,1)} %taps_hbm.1, f32[1,64]{1,0:T(1,128)} %bitcast.2), custom_call_target="tpu_custom_call" | custom-call | tf_op jit(solution)/shard_map/pallas_call | solution.py:470
  25.3 0.9 %shard_map.76 = (bf16[1,64,4,512]{3,2,1,0:T(4,128)(2,1)}, bf16[1,32,4,512]{3,2,1,0:T(4,128)(2,1)}, f32[27,2048]{1,0:T(8,128)}, f32[1,64]{1,0:T(1,128)}) custom-call(bf16[1,64,4,512]{3,2,1,0:T(4,128)(2,1)S(1)} %get-tuple-element.12.refs_0_, bf16[1,32,4,512]{3,2,1,0:T(4,128)(2,1)S(1)} %get-tuple-element.13.refs_1_, f32[27,2048]{1,0:T(8,128)S(1)} %get-tuple-element.14.refs_2_, ...), custom_call_target="tpu_custom_call" | custom-call | tf_op jit(solution)/shard_map/pallas_call | solution.py:490
